TPU v7x, 32 devices: a whole 2x2x4 slice. The times are simulated.
32 devices in a mesh: dp: 8 (over y, x, core), ctx: 4 (over z).
Axes of the slice: x: 2, y: 2, z: 4, core: 2. Of those that a mesh axis runs over, the one named last changes fastest.
Arguments:
- tokens: bfloat16 [64, 512, 1024], P('dp', 'ctx'), may hold values from -6 to 6
- lengths: int32 [64], P('dp'), may hold values from 128 to 512, as said below
- w_qkv: bfloat16 [1024, 3072], P('dp'), may hold values from -0.1875 to 0.1875
- bias_qv: bfloat16 [2048], P('dp'), may hold values from -3 to 3
- w_out: bfloat16 [1024, 1024], P('dp'), may hold values from -1.5 to 1.5
- bias_out: bfloat16 [1024], P('dp'), may hold values from -3 to 3
- gain_one: bfloat16 [1024], P('dp'), may hold values from 0.5 to 1.5
- shift_one: bfloat16 [1024], P('dp'), may hold values from -3 to 3
- w_up: bfloat16 [1024, 4096], P('dp'), may hold values from -0.1875 to 0.1875
- bias_up: bfloat16 [4096], P('dp'), may hold values from -3 to 3
- w_down: bfloat16 [4096, 1024], P('dp'), may hold values from -0.09375 to 0.09375
- bias_down: bfloat16 [1024], P('dp'), may hold values from -3 to 3
- gain_two: bfloat16 [1024], P('dp'), may hold values from 0.5 to 1.5
- shift_two: bfloat16 [1024], P('dp'), may hold values from -3 to 3
- cotangent: bfloat16 [64, 512, 1024], P('dp', 'ctx'), may hold values from -6 to 6
Outputs:
- output: bfloat16 [64, 512, 1024], P('dp', 'ctx')
- grad_input: float32 [64, 512, 1024], P('dp', 'ctx')
- grad_w_qkv: float32 [1024, 3072], P('dp')
- grad_bias_qv: float32 [2048], P('dp')
- grad_w_out: float32 [1024, 1024], P('dp')
- grad_bias_out: float32 [1024], P('dp')
- grad_gain_one: float32 [1024], P('dp')
- grad_shift_one: float32 [1024], P('dp')
- grad_w_up: float32 [1024, 4096], P('dp')
- grad_bias_up: float32 [4096], P('dp')
- grad_w_down: float32 [4096, 1024], P('dp')
- grad_bias_down: float32 [1024], P('dp')
- grad_gain_two: float32 [1024], P('dp')
- grad_shift_two: float32 [1024], P('dp')
Inputs may be any that keep to these rules, and one draw needn't show every extreme that they name: `lengths`: in each group of 8 slots that one index of dp holds, one slot has length 512 and another length 128.
All inputs are finite; a program needn't handle non-finite values.
Results may differ from a plain program's by a relative error of at most 0.017.
Values may be sent and summed in bfloat16 or wider, within the bound.
No kernel may reach another device: no remote copies, remote signals or barrier semaphores. Data moves between devices by JAX's collectives and lax.ppermute only.
A program may use at most 256 MiB of HBM per device.

v0:
```python
import jax
import jax.numpy as jnp
from jax import lax
from jax.sharding import PartitionSpec as P

HD = 64


neg_big = -1e30
eps_norm = 1e-06
head_group = 4


def layer_norm(rows, gain, shift):
    centre = rows - jnp.mean(rows, axis=-1, keepdims=True)
    inverse = lax.rsqrt(jnp.mean(centre * centre, axis=-1, keepdims=True) + eps_norm)
    normed = centre * inverse
    return (normed * gain + shift, normed, inverse)


def norm_back(grad_out, gain, normed, inverse):
    scaled = grad_out * gain
    return inverse * (
        scaled
        - jnp.mean(scaled, axis=-1, keepdims=True)
        - normed * jnp.mean(scaled * normed, axis=-1, keepdims=True)
    )


def contract_rows(left, right):
    return lax.dot_general(
        left, right, (((0,), (0,)), ((), ())), preferred_element_type=jnp.float32
    )


def times_transpose(left, right):
    return lax.dot_general(
        left, right, (((1,), (1,)), ((), ())), preferred_element_type=jnp.float32
    )


def split_groups(block, group):
    seqs, length, width = block.shape
    return jnp.moveaxis(block.reshape(seqs, length, width // (HD * group), group, HD), 2, 0)


def merge_groups(stacked):
    merged = jnp.moveaxis(stacked, 0, 2)
    return merged.reshape(merged.shape[0], merged.shape[1], -1)


def scores_of(queries, keys, valid):
    raw = jnp.einsum("sqhd,skhd->shqk", queries, keys, preferred_element_type=jnp.float32) * HD ** (
        -0.5
    )
    return jnp.where(valid[:, None, None, :], raw, neg_big)


def attend(pieces, valid):
    queries, keys, values = pieces
    masked = scores_of(queries, keys, valid)
    peak = jnp.max(masked, axis=-1, keepdims=True)
    weights = jnp.where(valid[:, None, None, :], jnp.exp(masked - peak), 0.0)
    total = jnp.sum(weights, axis=-1, keepdims=True)
    probs = (weights / total).astype(jnp.bfloat16)
    mixed = jnp.einsum("shqk,skhd->sqhd", probs, values, preferred_element_type=jnp.float32)
    return (mixed, peak, total)


def attend_back(pieces, valid):
    queries, keys, values, grad_mixed, peak, total = pieces
    masked = scores_of(queries, keys, valid)
    exact = jnp.where(valid[:, None, None, :], jnp.exp(masked - peak), 0.0) / total
    grad_probs = jnp.einsum(
        "sqhd,skhd->shqk", grad_mixed, values, preferred_element_type=jnp.float32
    )
    inner = jnp.sum(exact * grad_probs, axis=-1, keepdims=True)
    grad_scores = (exact * (grad_probs - inner)).astype(jnp.bfloat16)
    scale = HD ** (-0.5)
    grad_q = (
        jnp.einsum("shqk,skhd->sqhd", grad_scores, keys, preferred_element_type=jnp.float32) * scale
    )
    grad_k = (
        jnp.einsum("shqk,sqhd->skhd", grad_scores, queries, preferred_element_type=jnp.float32)
        * scale
    )
    grad_v = jnp.einsum(
        "shqk,sqhd->skhd",
        exact.astype(jnp.bfloat16),
        grad_mixed,
        preferred_element_type=jnp.float32,
    )
    return (grad_q, grad_k, grad_v)


def shards(
    tokens,
    lengths,
    w_qkv,
    bias_qv,
    w_out,
    bias_out,
    gain_one,
    shift_one,
    w_up,
    bias_up,
    w_down,
    bias_down,
    gain_two,
    shift_two,
    cotangent,
):
    (
        qkv_full,
        bqv_full,
        out_full,
        bout_full,
        gone_full,
        sone_full,
        up_full,
        bup_full,
        down_full,
        bdown_full,
        gtwo_full,
        stwo_full,
    ) = (
        lax.all_gather(w_qkv, "dp", axis=0, tiled=True),
        lax.all_gather(bias_qv, "dp", axis=0, tiled=True),
        lax.all_gather(w_out, "dp", axis=0, tiled=True),
        lax.all_gather(bias_out, "dp", axis=0, tiled=True),
        lax.all_gather(gain_one, "dp", axis=0, tiled=True),
        lax.all_gather(shift_one, "dp", axis=0, tiled=True),
        lax.all_gather(w_up, "dp", axis=0, tiled=True),
        lax.all_gather(bias_up, "dp", axis=0, tiled=True),
        lax.all_gather(w_down, "dp", axis=0, tiled=True),
        lax.all_gather(bias_down, "dp", axis=0, tiled=True),
        lax.all_gather(gain_two, "dp", axis=0, tiled=True),
        lax.all_gather(shift_two, "dp", axis=0, tiled=True),
    )
    bqv = bqv_full.astype(jnp.float32)
    bout = bout_full.astype(jnp.float32)
    gone = gone_full.astype(jnp.float32)
    sone = sone_full.astype(jnp.float32)
    bup = bup_full.astype(jnp.float32)
    bdown = bdown_full.astype(jnp.float32)
    gtwo = gtwo_full.astype(jnp.float32)
    stwo = stwo_full.astype(jnp.float32)
    seqs, blk, width = tokens.shape
    group = min(head_group, width // HD)
    place = lax.axis_index("ctx")
    slot = blk * lax.axis_size("ctx")
    query_pos = place * blk + jnp.arange(blk, dtype=jnp.int32)
    own_valid = query_pos[None, :] < lengths[:, None]
    row_valid = own_valid.astype(jnp.float32).reshape(seqs * blk, 1)
    key_valid = jnp.arange(slot, dtype=jnp.int32)[None, :] < lengths[:, None]
    rows = tokens.reshape(seqs * blk, width)
    zero_bias = jnp.zeros((width,), jnp.float32)
    projected = jnp.dot(rows, qkv_full, preferred_element_type=jnp.float32) + jnp.concatenate(
        [bqv[:width], zero_bias, bqv[width:]]
    )
    projected = projected.astype(jnp.bfloat16)
    queries = projected[:, :width].reshape(seqs, blk, width)
    keys = projected[:, width : 2 * width].reshape(seqs, blk, width)
    values = projected[:, 2 * width :].reshape(seqs, blk, width)
    all_keys, all_values = (
        lax.all_gather(keys, "ctx", axis=1, tiled=True),
        lax.all_gather(values, "ctx", axis=1, tiled=True),
    )
    query_groups = split_groups(queries, group)
    key_groups = split_groups(all_keys, group)
    value_groups = split_groups(all_values, group)
    mixed, peak, total = lax.map(
        lambda pieces: attend(pieces, key_valid), (query_groups, key_groups, value_groups)
    )
    attn_rows = merge_groups(mixed).reshape(seqs * blk, width).astype(jnp.bfloat16)
    branch = jnp.dot(attn_rows, out_full, preferred_element_type=jnp.float32) + bout
    first, normed_one, inverse_one = layer_norm(rows.astype(jnp.float32) + branch, gone, sone)
    first_low = first.astype(jnp.bfloat16)
    hidden_pre = jnp.dot(first_low, up_full, preferred_element_type=jnp.float32) + bup
    active_low = jax.nn.gelu(hidden_pre, approximate=False).astype(jnp.bfloat16)
    second = jnp.dot(active_low, down_full, preferred_element_type=jnp.float32) + bdown
    result, normed_two, inverse_two = layer_norm(first + second, gtwo, stwo)
    output = (result * row_valid).astype(jnp.bfloat16).reshape(seqs, blk, width)
    qkv_back, out_back, up_back, down_back = (
        lax.all_gather(w_qkv, "dp", axis=0, tiled=True),
        lax.all_gather(w_out, "dp", axis=0, tiled=True),
        lax.all_gather(w_up, "dp", axis=0, tiled=True),
        lax.all_gather(w_down, "dp", axis=0, tiled=True),
    )
    grad_result = cotangent.reshape(seqs * blk, width).astype(jnp.float32) * row_valid
    grad_gain_two = jnp.sum(grad_result * normed_two, axis=0)
    grad_shift_two = jnp.sum(grad_result, axis=0)
    grad_sum_two = norm_back(grad_result, gtwo, normed_two, inverse_two)
    grad_second = grad_sum_two.astype(jnp.bfloat16)
    grad_bias_down = jnp.sum(grad_second, axis=0, dtype=jnp.float32)
    grad_down = contract_rows(active_low, grad_second)
    grad_active = times_transpose(grad_second, down_back)
    unused_value, gelu_back = jax.vjp(lambda pre: jax.nn.gelu(pre, approximate=False), hidden_pre)
    grad_hidden = gelu_back(grad_active)[0].astype(jnp.bfloat16)
    grad_up = contract_rows(first_low, grad_hidden)
    grad_bias_up = jnp.sum(grad_hidden, axis=0, dtype=jnp.float32)
    grad_first = grad_sum_two + times_transpose(grad_hidden, up_back)
    grad_gain_one = jnp.sum(grad_first * normed_one, axis=0)
    grad_shift_one = jnp.sum(grad_first, axis=0)
    grad_sum_one = norm_back(grad_first, gone, normed_one, inverse_one)
    grad_branch = grad_sum_one.astype(jnp.bfloat16)
    grad_bias_out = jnp.sum(grad_branch, axis=0, dtype=jnp.float32)
    grad_out = contract_rows(attn_rows, grad_branch)
    grad_mixed = (
        times_transpose(grad_branch, out_back).astype(jnp.bfloat16).reshape(seqs, blk, width)
    )
    grad_mixed_groups = split_groups(grad_mixed, group)
    grad_q_groups, grad_k_groups, grad_v_groups = lax.map(
        lambda pieces: attend_back(pieces, key_valid),
        (query_groups, key_groups, value_groups, grad_mixed_groups, peak, total),
    )
    grad_queries = merge_groups(grad_q_groups).reshape(seqs * blk, width)
    grad_keys_all = merge_groups(grad_k_groups)
    grad_values_all = merge_groups(grad_v_groups)
    grad_keys, grad_values = (
        lax.psum_scatter(
            grad_keys_all.astype(jnp.bfloat16), "ctx", scatter_dimension=1, tiled=True
        ).astype(jnp.float32),
        lax.psum_scatter(
            grad_values_all.astype(jnp.bfloat16), "ctx", scatter_dimension=1, tiled=True
        ).astype(jnp.float32),
    )
    grad_proj = jnp.concatenate(
        [
            grad_queries,
            grad_keys.reshape(seqs * blk, width),
            grad_values.reshape(seqs * blk, width),
        ],
        axis=1,
    ).astype(jnp.bfloat16)
    grad_qkv = contract_rows(rows, grad_proj)
    grad_bias_qv = jnp.concatenate(
        [
            jnp.sum(grad_proj[:, :width], axis=0, dtype=jnp.float32),
            jnp.sum(grad_proj[:, 2 * width :], axis=0, dtype=jnp.float32),
        ]
    )
    grad_input = grad_sum_one + times_transpose(grad_proj, qkv_back)
    (
        share_qkv,
        share_bias_qv,
        share_out,
        share_bias_out,
        share_gain_one,
        share_shift_one,
        share_up,
        share_bias_up,
        share_down,
        share_bias_down,
        share_gain_two,
        share_shift_two,
    ) = (
        lax.psum_scatter(grad_qkv, "dp", scatter_dimension=0, tiled=True),
        lax.psum_scatter(grad_bias_qv, "dp", scatter_dimension=0, tiled=True),
        lax.psum_scatter(grad_out, "dp", scatter_dimension=0, tiled=True),
        lax.psum_scatter(grad_bias_out, "dp", scatter_dimension=0, tiled=True),
        lax.psum_scatter(grad_gain_one, "dp", scatter_dimension=0, tiled=True),
        lax.psum_scatter(grad_shift_one, "dp", scatter_dimension=0, tiled=True),
        lax.psum_scatter(grad_up, "dp", scatter_dimension=0, tiled=True),
        lax.psum_scatter(grad_bias_up, "dp", scatter_dimension=0, tiled=True),
        lax.psum_scatter(grad_down, "dp", scatter_dimension=0, tiled=True),
        lax.psum_scatter(grad_bias_down, "dp", scatter_dimension=0, tiled=True),
        lax.psum_scatter(grad_gain_two, "dp", scatter_dimension=0, tiled=True),
        lax.psum_scatter(grad_shift_two, "dp", scatter_dimension=0, tiled=True),
    )
    summed = (
        lax.psum(share_qkv.astype(jnp.bfloat16), "ctx").astype(jnp.float32),
        lax.psum(share_bias_qv.astype(jnp.bfloat16), "ctx").astype(jnp.float32),
        lax.psum(share_out.astype(jnp.bfloat16), "ctx").astype(jnp.float32),
        lax.psum(share_bias_out.astype(jnp.bfloat16), "ctx").astype(jnp.float32),
        lax.psum(share_gain_one.astype(jnp.bfloat16), "ctx").astype(jnp.float32),
        lax.psum(share_shift_one.astype(jnp.bfloat16), "ctx").astype(jnp.float32),
        lax.psum(share_up.astype(jnp.bfloat16), "ctx").astype(jnp.float32),
        lax.psum(share_bias_up.astype(jnp.bfloat16), "ctx").astype(jnp.float32),
        lax.psum(share_down.astype(jnp.bfloat16), "ctx").astype(jnp.float32),
        lax.psum(share_bias_down.astype(jnp.bfloat16), "ctx").astype(jnp.float32),
        lax.psum(share_gain_two.astype(jnp.bfloat16), "ctx").astype(jnp.float32),
        lax.psum(share_shift_two.astype(jnp.bfloat16), "ctx").astype(jnp.float32),
    )
    return (
        output,
        grad_input.reshape(seqs, blk, width),
        summed[0],
        summed[1],
        summed[2],
        summed[3],
        summed[4],
        summed[5],
        summed[6],
        summed[7],
        summed[8],
        summed[9],
        summed[10],
        summed[11],
    )


def solution(mesh):
    return jax.shard_map(
        shards,
        mesh=mesh,
        in_specs=(
            P("dp", "ctx", None),
            P("dp"),
            P("dp", None),
            P("dp"),
            P("dp", None),
            P("dp"),
            P("dp"),
            P("dp"),
            P("dp", None),
            P("dp"),
            P("dp", None),
            P("dp"),
            P("dp"),
            P("dp"),
            P("dp", "ctx", None),
        ),
        out_specs=(
            P("dp", "ctx", None),
            P("dp", "ctx", None),
            P("dp", None),
            P("dp"),
            P("dp", None),
            P("dp"),
            P("dp"),
            P("dp"),
            P("dp", None),
            P("dp"),
            P("dp", None),
            P("dp"),
            P("dp"),
            P("dp"),
        ),
        check_vma=False,
    )
```

profile of v0, /device:TPU:0, one launch (start us, length us, event | category | flops | bytes accessed | tf_op | source)
XLA Modules:
  0.0 1521.2 jit_solution(7666984952614874113)
XLA Ops:
  19.0 39.2 %all-gather.15.cloned.1.call-done = bf16[1024,3072]{1,0:T(8,128)(2,1)} async-done(((bf16[128,3072]{1,0:T(8,128)(2,1)}), bf16[1024,3072]{1,0:T(8,128)(2,1)}) %all-gather.15.cloned.1.call-update) | async-done | bytes 6291472 | tf_op jit(solution)/shard_map/all_gather | solution.py:127
  146.6 75.3 %all-gather.17.cloned.1.call-done = bf16[8,512,1024]{1,2,0:T(8,128)(2,1)} async-done(((bf16[8,128,1024]{1,2,0:T(8,128)(2,1)}), bf16[8,512,1024]{1,2,0:T(8,128)(2,1)}) %all-gather.17.cloned.1.call-update) | async-done | bytes 8388624 | tf_op jit(solution)/shard_map/all_gather | solution.py:167
  229.9 141.6 %all-gather.19.cloned.1.call-done = bf16[8,512,1024]{1,2,0:T(8,128)(2,1)} async-done(((bf16[8,128,1024]{1,2,0:T(8,128)(2,1)}), bf16[8,512,1024]{1,2,0:T(8,128)(2,1)}) %all-gather.19.cloned.1.call-update) | async-done | bytes 8388624 | tf_op jit(solution)/shard_map/all_gather | solution.py:166
  379.7 43.2 %while.30 = (s32[]{:T(128)}, bf16[4,8,128,4,64]{2,4,3,1,0:T(8,128)(2,1)S(1)}, f32[4,8,4,128,1]{3,2,1,4,0:T(4,128)}, f32[4,8,4,128,1]{3,2,1,4,0:T(4,128)}, bf16[4...) while((s32[]{:T(128)}, ...), condition=%wide.region_3.4_spmd.clone, body=%wide.region_0.3_spmd.clone.sunk | while | flops 566226944 | bytes 31099516 | solution.py:172
  434.3 21.2 %all-gather.23.cloned.1.call-done = bf16[1024,4096]{1,0:T(8,128)(2,1)} async-done(((bf16[128,4096]{1,0:T(8,128)(2,1)}), bf16[1024,4096]{1,0:T(8,128)(2,1)}) %all-gather.23.cloned.1.call-update) | async-done | bytes 8388624 | tf_op jit(solution)/shard_map/all_gather | solution.py:133
  455.5 51.3 %multiply_convert_fusion.1 = (bf16[1024,4096]{1,0:T(8,128)(2,1)}, f32[1024,4096]{1,0:T(8,128)}, f32[1024,4096]{1,0:T(8,128)}) fusion(f32[4096]{0:T(1024)S(1)} %bitcast.284, bf16[1024,4096]{1,0:T(8,128)(2,1)} %all-gather.23.cloned.1.call-done, f32[1024,1024]{1,0:T(8,128)} %copy-done.3, f32[1024]{0:T(1024)S(1)} %bitcast.288, f32[1024]{0:T(1024)S(1)} %bitcast.278, ...), kind=kOutput, calls=%fused_computation.60 | convolution fusion | flops 8872001536 | bytes 54558720 | tf_op jit(solution)/shard_map/dot_general | solution.py:179
  511.7 14.8 fusion.88
  535.3 24.8 %convert_reduce_fusion = (f32[4096]{0:T(1024)}, bf16[1024,4096]{1,0:T(8,128)(2,1)}) fusion(f32[1024,4096]{1,0:T(8,128)} %get-tuple-element.318, bf16[4096,1024]{1,0:T(8,128)(2,1)} %all-gather.25.cloned.1.call-done, f32[1024,1024]{1,0:T(8,128)} %get-tuple-element.314, f32[1024,4096]{1,0:T(8,128)} %get-tuple-element.337, f32[4096]{0:T(1024)S(1)} %bitcast.285), kind=kOutput, calls=%fused_computation.58 | convolution fusion | flops 8662282240 | bytes 54558720 | tf_op jit(solution)/shard_map/dot_general | solution.py:37
  560.1 17.5 %multiply_reduce_fusion.2 = (f32[1024]{0:T(1024)}, f32[1024]{0:T(1024)S(1)}, f32[1024]{0:T(1024)S(1)}, f32[1024]{0:T(1024)}, f32[1024,1024]{1,0:T(8,128)S(1)}) fusion(f32[1024,1024]{1,0:T(8,128)} %copy-done.3, f32[1024]{0:T(1024)S(1)} %add_rsqrt_fusion.1, f32[1024]{0:T(1024)S(1)} %broadcast_multiply_fusion.4, f32[1024]{0:T(1024)S(1)} %bitcast.280, ...), kind=kOutput, calls=%fused_computation.79 | convolution fusion | flops 8600416256 | bytes 29388800 | tf_op jit(solution)/shard_map/dot_general | solution.py:37
  592.2 74.9 %while.31 = (s32[]{:T(128)}, bf16[4,8,128,4,64]{2,4,3,1,0:T(8,128)(2,1)}, bf16[4,8,512,4,64]{2,4,3,0,1:T(8,128)(2,1)}, bf16[4,8,512,4,64]{2,4,3,0,1:T(8,128)(2,1...) while((s32[]{:T(128)}, ...), condition=%wide.region_14.15_spmd.clone, body=%wide.region_12.14_spmd.clone.sunk | while | flops 1366556672 | bytes 107098312 | solution.py:213
  680.0 16.4 %copy.100 = bf16[64,8,8,1024]{3,1,2,0:T(8,128)(2,1)} copy(bf16[64,8,8,1024]{3,2,1,0:T(8,128)(2,1)} %bitcast.251) | data formatting | bytes 16777216
  709.3 16.4 %copy.103 = bf16[64,8,8,1024]{3,1,2,0:T(8,128)(2,1)} copy(bf16[64,8,8,1024]{3,2,1,0:T(8,128)(2,1)} %bitcast.252) | data formatting | bytes 16777216
  734.5 16.8 %fusion.80 = f32[1024,4096]{1,0:T(8,128)} fusion(bf16[1024,4096]{1,0:T(8,128)(2,1)} %get-tuple-element.342, f32[1024,1024]{1,0:T(8,128)} %copy-done.3, f32[1024]{0:T(1024)S(1)} %bitcast.290, f32[1024]{0:T(1024)S(1)} %bitcast.282, f32[1024]{0:T(1024)S(1)} %copy-done.23, f32[1024]{0:T(1024)S(1)} %copy-done.15), kind=kOutput, calls=%fused_computation.142 | convolution fusion | flops 8595177472 | bytes 29376512 | tf_op jit(solution)/shard_map/dot_general | solution.py:31
  751.5 16.5 %fusion.74 = f32[4096,1024]{1,0:T(8,128)} fusion(bf16[1024,4096]{1,0:T(8,128)(2,1)} %get-tuple-element.317, f32[1024,1024]{1,0:T(8,128)} %get-tuple-element.314), kind=kOutput, calls=%fused_computation.138 | convolution fusion | flops 8590983168 | bytes 29360128 | tf_op jit(solution)/shard_map/dot_general | solution.py:31
  773.7 67.3 %reduce-scatter.19.cloned.1.call-done = bf16[128,8192]{1,0:T(8,128)(2,1)} async-done(((bf16[512,8192]{1,0:T(8,128)(2,1)}), bf16[128,8192]{1,0:T(8,128)(2,1)}) %reduce-scatter.19.cloned.1.call-update) | async-done | bytes 2097168
  849.8 138.8 %reduce-scatter.21.cloned.1.call-done = bf16[128,8192]{1,0:T(8,128)(2,1)} async-done(((bf16[512,8192]{1,0:T(8,128)(2,1)}), bf16[128,8192]{1,0:T(8,128)(2,1)}) %reduce-scatter.21.cloned.1.call-update) | async-done | bytes 2097168
  1002.9 13.1 convolution_bitcast_fusion
  1016.1 27.9 %reduce-scatter.13.cloned.1.call-done = f32[128,1024]{1,0:T(8,128)} async-done(((f32[1024,1024]{1,0:T(8,128)}), f32[128,1024]{1,0:T(8,128)}) %reduce-scatter.13.cloned.1.call-update) | async-done | bytes 524304 | tf_op jit(solution)/shard_map/reduce_scatter | solution.py:260
  1045.8 118.0 %reduce-scatter.15.cloned.1.call-done = f32[128,4096]{1,0:T(8,128)} async-done(((f32[1024,4096]{1,0:T(8,128)}), f32[128,4096]{1,0:T(8,128)}) %reduce-scatter.15.cloned.1.call-update) | async-done | bytes 2097168 | tf_op jit(solution)/shard_map/reduce_scatter | solution.py:264
  1166.5 117.3 %reduce-scatter.17.cloned.1.call-done = f32[512,1024]{1,0:T(8,128)} async-done(((f32[4096,1024]{1,0:T(8,128)}), f32[512,1024]{1,0:T(8,128)}) %reduce-scatter.17.cloned.1.call-update) | async-done | bytes 2097168 | tf_op jit(solution)/shard_map/reduce_scatter | solution.py:266
  1286.5 93.5 %reduce-scatter.11.cloned.1.call-done = f32[128,3072]{0,1:T(8,128)} async-done(((f32[1024,3072]{0,1:T(8,128)}), f32[128,3072]{0,1:T(8,128)}) %reduce-scatter.11.cloned.1.call-update) | async-done | bytes 1572880 | tf_op jit(solution)/shard_map/reduce_scatter | solution.py:258
  1387.0 25.0 %all-reduce.8 = (bf16[2048]{0:T(1024)(128)(2,1)S(1)}, bf16[1024]{0:T(1024)(128)(2,1)S(1)}, bf16[1024]{0:T(1024)(128)(2,1)S(1)}, bf16[1024]{0:T(1024)(128)(2,1)S(...) all-reduce(f32[2048]{0:T(1024)S(1)} %pad_maximum_fusion.1, ...), channel_id=5, replica_groups=mesh['dp'=8,'ctx'=4] {'dp'}, use_global_device_ids=true, to_apply=%region_21.22.clone | all-reduce | flops 12288 | bytes 73728
  1412.7 13.1 all-reduce.9
  1442.7 63.9 %all-reduce.13.cloned.1.call-done = (bf16[128,3072]{0,1:T(8,128)(2,1)}, bf16[128,1024]{1,0:T(8,128)(2,1)}, bf16[128,4096]{1,0:T(8,128)(2,1)}, bf16[512,1024]{1,0:T(8,128)(2,1)}) async-done(((bf16[128,3072]{0,1:T(8,128)(2,1)}, bf16[128,1024]{1,0:T(8,128)(2,1)}, bf16[128,4096]{1,0:T(8,128)(2,1)}, bf16[512,1024]{1,0:T(8,128)(2,1)}), (bf16[128,3072]{0,1:T(8,128)(2,1)}, bf16[128,1024]{1,0:T(8,128)(2,1)}, ...) | async-done | bytes 3145744 | tf_op jit(solution)/shard_map/psum | solution.py:272
  (283 shorter events, 374.9 us)
Async XLA Ops:
  7.2 51.0 %all-gather.15.cloned.1.call-start = ((), (), s32[]{:S(2)}) async-start(), calls=%async_computation.6 | async-start | bytes 7077888 | tf_op jit(solution)/shard_map/all_gather | solution.py:127
  7.9 214.1 %all-gather.17.cloned.1.call-start = ((), (), s32[]{:S(2)}) async-start(), calls=%async_computation.7 | async-start | bytes 10485760 | tf_op jit(solution)/shard_map/all_gather | solution.py:167
  72.7 298.8 %all-gather.19.cloned.1.call-start = ((), (), s32[]{:S(2)}) async-start(), calls=%async_computation.8 | async-start | bytes 10485760 | tf_op jit(solution)/shard_map/all_gather | solution.py:166
  72.8 39.2 %copy-start.36 = (bf16[128]{0:T(256)(128)(2,1)S(1)}, bf16[128]{0:T(256)(128)(2,1)}, u32[]{:S(2)}) copy-start(bf16[128]{0:T(256)(128)(2,1)} %param.30) | copy-start | bytes 772
  72.8 48.5 %copy-start.37 = (bf16[128]{0:T(256)(128)(2,1)S(1)}, bf16[128]{0:T(256)(128)(2,1)}, u32[]{:S(2)}) copy-start(bf16[128]{0:T(256)(128)(2,1)} %param.31) | copy-start | bytes 772
  72.8 56.3 %copy-start.11 = (s32[8]{0:T(128)S(1)}, s32[8]{0:T(128)}, u32[]{:S(2)}) copy-start(s32[8]{0:T(128)} %param.20) | copy-start | bytes 100
  72.8 56.9 %copy-start.1 = (bf16[8,128,1024]{2,1,0:T(8,128)(2,1)S(1)}, bf16[8,128,1024]{2,1,0:T(8,128)(2,1)}, u32[]{:S(2)}) copy-start(bf16[8,128,1024]{2,1,0:T(8,128)(2,1)} %param.33) | copy-start | bytes 6291460
  76.9 54.8 %copy-start.38 = (bf16[128]{0:T(256)(128)(2,1)S(1)}, bf16[128]{0:T(256)(128)(2,1)}, u32[]{:S(2)}) copy-start(bf16[128]{0:T(256)(128)(2,1)} %param.32) | copy-start | bytes 772
  76.9 349.1 %all-gather.21.cloned.1.call-start = ((), (), s32[]{:S(2)}) async-start(), calls=%async_computation.9 | async-start | bytes 2359296 | tf_op jit(solution)/shard_map/all_gather | solution.py:129
  77.5 378.0 %all-gather.23.cloned.1.call-start = ((), (), s32[]{:S(2)}) async-start(), calls=%async_computation.10 | async-start | bytes 9437184 | tf_op jit(solution)/shard_map/all_gather | solution.py:133
  78.1 433.6 %all-gather.25.cloned.1.call-start = ((), (), s32[]{:S(2)}) async-start(), calls=%async_computation.11 | async-start | bytes 9437184 | tf_op jit(solution)/shard_map/all_gather | solution.py:135
  78.7 762.3 %reduce-scatter.19.cloned.1.call-start = ((), (), s32[]{:S(2)}) async-start(), calls=%async_computation.16 | async-start | bytes 10485760
  95.3 482.3 %copy-start.20 = (f32[8,1,128]{2,1,0:T(1,128)}, f32[8,1,128]{2,1,0:T(1,128)S(1)}, u32[]{:S(2)}) copy-start(f32[8,1,128]{2,1,0:T(1,128)S(1)} %convert_element_type.265) | copy-start | bytes 12292
  104.0 407.7 %copy-start.29 = (f32[8,1,128]{2,1,0:T(1,128)}, f32[8,1,128]{2,1,0:T(1,128)S(1)}, u32[]{:S(2)}) copy-start(f32[8,1,128]{2,1,0:T(1,128)S(1)} %convert_element_type.266) | copy-start | bytes 12292
  431.7 145.8 %copy-start.14 = (f32[1024]{0:T(1024)}, f32[1024]{0:T(1024)S(1)}, u32[]{:S(2)}) copy-start(f32[1024]{0:T(1024)S(1)} %broadcast_multiply_fusion.4) | copy-start | bytes 12292
  434.3 143.3 %copy-start.22 = (f32[1024]{0:T(1024)}, f32[1024]{0:T(1024)S(1)}, u32[]{:S(2)}) copy-start(f32[1024]{0:T(1024)S(1)} %add_rsqrt_fusion.1) | copy-start | bytes 12292
  455.5 56.2 %copy-start.31 = (f32[8,1,128]{2,1,0:T(1,128)S(1)}, f32[8,1,128]{2,1,0:T(1,128)}, u32[]{:S(2)}) copy-start(f32[8,1,128]{2,1,0:T(1,128)} %convert_element_type.268) | copy-start | bytes 12292
  696.4 292.2 %reduce-scatter.21.cloned.1.call-start = ((), (), s32[]{:S(2)}) async-start(), calls=%async_computation.17 | async-start | bytes 10485760
  725.8 318.2 %reduce-scatter.13.cloned.1.call-start = ((), (), s32[]{:S(2)}) async-start(), calls=%async_computation.13 | async-start | bytes 4718592 | tf_op jit(solution)/shard_map/reduce_scatter | solution.py:260
  733.9 429.9 %reduce-scatter.15.cloned.1.call-start = ((), (), s32[]{:S(2)}) async-start(), calls=%async_computation.14 | async-start | bytes 18874368 | tf_op jit(solution)/shard_map/reduce_scatter | solution.py:264
  751.4 532.4 %reduce-scatter.17.cloned.1.call-start = ((), (), s32[]{:S(2)}) async-start(), calls=%async_computation.15 | async-start | bytes 18874368 | tf_op jit(solution)/shard_map/reduce_scatter | solution.py:266
  768.0 612.0 %reduce-scatter.11.cloned.1.call-start = ((), (), s32[]{:S(2)}) async-start(), calls=%async_computation.12 | async-start | bytes 14155776 | tf_op jit(solution)/shard_map/reduce_scatter | solution.py:258
  1016.0 490.6 %all-reduce.13.cloned.1.call-start = ((), (), s32[]{:S(2)}) async-start(), calls=%async_computation.18 | async-start | bytes 6291456 | tf_op jit(solution)/shard_map/psum | solution.py:272
  1166.5 215.9 %copy-start.41 = (u32[32]{0:T(128)S(1)}, u32[32]{0:T(128)}, u32[]{:S(2)}) copy-start(u32[32]{0:T(128)} %constant.136) | copy-start | bytes 388
  (39 other events, 224.2 us)
Sparse Core Ops, SparseCore 0:
  9.9 48.2 all-gather.14
  72.8 149.1 all-gather.16
  224.1 147.3 all-gather.18
  373.2 26.0 all-gather.20
  401.1 54.3 all-gather.22
  457.2 54.3 all-gather.24
  696.5 144.4 reduce-scatter.18
  843.3 145.1 reduce-scatter.20
  991.9 52.0 reduce-scatter.12
  1047.8 115.9 reduce-scatter.14
  1167.8 115.9 reduce-scatter.16
  1287.5 92.3 reduce-scatter.10
  1383.9 122.6 all-reduce.12
where the time goes:
time: 1530 us; the launch traced here: 1520 us
  waiting for transfers between devices  911 us (60%)
  matrix products  286 us (19%)
  local copies, waits for them, and re-layouts  148 us (10%)
  blocking collectives  107 us (7%)
  other arithmetic  50.4 us (3%)
  between operations  16.6 us (1%)
    unnamed x15, waiting for transfers between devices  208 us
    all_gather x1, waiting for transfers between devices, shards(): lax.all_gather(keys, 'ctx', axis=1, tiled=True)  142 us
    reduce_scatter x1, waiting for transfers between devices, shards(): lax.psum_scatter(grad_up, 'dp', scatter_dimension=0, tiled=True)  118 us
    reduce_scatter x1, waiting for transfers between devices, shards(): lax.psum_scatter(grad_down, 'dp', scatter_dimension=0, tiled=True)  117 us
    unnamed x109, local copies, waits for them, and re-layouts  103 us
    reduce_scatter x1, waiting for transfers between devices, shards(): lax.psum_scatter(grad_qkv, 'dp', scatter_dimension=0, tiled=True)  93.5 us
    all_gather x1, waiting for transfers between devices, shards(): lax.all_gather(values, 'ctx', axis=1, tiled=True)  75.3 us
    psum x1, waiting for transfers between devices, shards(): lax.psum(share_qkv.astype(jnp.bfloat16), 'ctx').astype(jnp.float32)  63.9 us
  transfers between devices with their start and end apart: 13, of which 12 were waited for; matrix products, arithmetic and copies ran while one was open for 18% of the time, Pallas kernels for 0%

commit v1 on v0

v1 whole, which is shorter than its diff:
```python
import functools

import jax
import jax.numpy as jnp
from jax import lax
from jax.experimental import pallas as pl
from jax.experimental.pallas import tpu as pltpu
from jax.sharding import PartitionSpec as P

HD = 64
NEG = -1e30
EPS = 1e-06
BF = jnp.bfloat16
F32 = jnp.float32
MIB = 1024 * 1024
ANY = pl.BlockSpec(memory_space=pl.ANY)


def swap(x, axis, bit):
    n = lax.axis_size(axis)
    return lax.ppermute(x, axis, [(i, i ^ bit) for i in range(n)])


def gather_dp(own):
    n = lax.axis_size("dp")
    if n == 8:
        half = own.shape[1] // 2
        at_x = swap(own, "dp", 2)
        at_y = swap(own, "dp", 4)
        left = swap(at_x[:, :half], "dp", 4)
        right = swap(at_y[:, half:], "dp", 2)
        mine = jnp.stack([own, at_x, at_y, jnp.concatenate([left, right], axis=1)])
    else:
        mine = own[None]
        bit = 2
        while bit < n:
            mine = jnp.concatenate([mine, swap(mine, "dp", bit)])
            bit *= 2
    return mine, swap(mine, "dp", 1)


def add_low(*parts):
    total = parts[0].astype(F32)
    for part in parts[1:]:
        total = total + part.astype(F32)
    return total.astype(BF)


def reduce_dp(grad):
    n = lax.axis_size("dp")
    me = lax.axis_index("dp")
    rows = grad.shape[0] // n
    width = grad.shape[1]

    def shard(rel):
        return lax.dynamic_slice(grad, ((me ^ rel) * rows, 0), (rows, width))

    away = jnp.stack([shard(2 * k + 1) for k in range(n // 2)])
    come = swap(away, "dp", 1)
    if n == 8:
        half = width // 2
        own, to_x, to_y, to_xy = (add_low(shard(2 * k), come[k]) for k in range(4))
        left = swap(to_xy[:, :half], "dp", 4)
        right = swap(to_xy[:, half:], "dp", 2)
        to_x = jnp.concatenate([add_low(to_x[:, :half], left), to_x[:, half:]], axis=1)
        to_y = jnp.concatenate([to_y[:, :half], add_low(to_y[:, half:], right)], axis=1)
        return add_low(own, swap(to_x, "dp", 2), swap(to_y, "dp", 4))
    mine = add_low(jnp.stack([shard(2 * k) for k in range(n // 2)]), come)
    bit = n // 2
    while bit > 1:
        keep = mine.shape[0] // 2
        mine = add_low(mine[:keep], swap(mine[keep:], "dp", bit))
        bit //= 2
    return mine[0]


def sum_ctx(share):
    n = lax.axis_size("ctx")
    if n != 4:
        return lax.psum(share.astype(F32), "ctx")
    inner = add_low(share, lax.ppermute(share, "ctx", [(0, 1), (3, 2)]))
    total = add_low(inner, lax.ppermute(inner, "ctx", [(1, 2), (2, 1)]))
    outer = lax.ppermute(total, "ctx", [(1, 0), (2, 3)])
    place = lax.axis_index("ctx")
    return jnp.where((place == 0) | (place == 3), outer, total).astype(F32)


def to_sequences(block, order):
    n = lax.axis_size("ctx")
    me = lax.axis_index("ctx")
    per = block.shape[0] // n

    def part(j):
        return lax.dynamic_slice_in_dim(block, (me ^ j) * per, per, axis=0)

    return jnp.stack([part(0)] + [swap(part(j), "ctx", j) for j in range(1, n)])


def from_sequences(parts, dtype):
    n = lax.axis_size("ctx")
    me = lax.axis_index("ctx")
    per = parts.shape[1]
    out = jnp.zeros((n * per,) + parts.shape[2:], dtype)
    for j in range(n):
        piece = parts[j] if j == 0 else swap(parts[j], "ctx", j)
        out = lax.dynamic_update_slice_in_dim(out, piece.astype(dtype), (me ^ j) * per, axis=0)
    return out


def nn(left, right):
    return jnp.dot(left, right, preferred_element_type=F32)


def nt(left, right):
    return lax.dot_general(left, right, (((1,), (1,)), ((), ())), preferred_element_type=F32)


def tn(left, right):
    return lax.dot_general(left, right, (((0,), (0,)), ((), ())), preferred_element_type=F32)


def fold(rows):
    return jnp.sum(rows.reshape(rows.shape[0] // 8, 8, rows.shape[1]), axis=0)


def fetch(stacks, whole, sems, me):
    copies = []
    for odd, stack in enumerate(stacks):
        count, rows, _ = stack.shape
        for k in range(count):
            start = pl.multiple_of((me ^ (2 * k + odd)) * rows, rows)
            copies.append(
                pltpu.make_async_copy(
                    stack.at[k], whole.at[pl.ds(start, rows)], sems.at[odd * count + k]
                )
            )
    for copy in copies:
        copy.start()
    for copy in copies:
        copy.wait()


def row_spec(tile, width):
    return pl.BlockSpec((tile, width), lambda i, *_: (i, 0))


def one_spec(height, width):
    return pl.BlockSpec((height, width), lambda i, *_: (0, 0))


def dense(body, name, meta, rows, tile, row_ins, vec_ins, weights, row_outs, sums, flops):
    stacks = [s for pair in weights for s in pair]
    scratch = []
    for mine, other in weights:
        count, r, width = mine.shape
        scratch.append(pltpu.VMEM((2 * count * r, width), BF))
        scratch.append(pltpu.SemaphoreType.DMA((2 * count,)))
    n_row, n_vec, n_stack = len(row_ins), len(vec_ins), len(stacks)
    n_out, n_sum = len(row_outs), len(sums)

    def kernel(meta_ref, *refs):
        pos = 0
        groups = []
        for count in (n_row, n_vec, n_stack, n_out, n_sum, 2 * len(weights)):
            groups.append(refs[pos : pos + count])
            pos += count
        row_refs, vec_refs, stack_refs, out_refs, sum_refs, scratch_refs = groups

        @pl.when(pl.program_id(0) == 0)
        def _():
            for w in range(len(weights)):
                fetch(stack_refs[2 * w : 2 * w + 2], scratch_refs[2 * w], scratch_refs[2 * w + 1], meta_ref[0])
            for ref in sum_refs:
                ref[...] = jnp.zeros_like(ref)

        body(meta_ref, row_refs, vec_refs, scratch_refs[::2], out_refs, sum_refs)

    in_specs = (
        [row_spec(tile, a.shape[-1]) if a.ndim == 2 else pl.BlockSpec((a.shape[0], tile, a.shape[2]), lambda i, *_: (0, i, 0)) for a in row_ins]
        + [one_spec(1, v.shape[1]) for v in vec_ins]
        + [ANY] * n_stack
    )
    out_specs = [row_spec(tile, w) for w, _ in row_outs] + [one_spec(8, w) for w in sums]
    out_shape = [jax.ShapeDtypeStruct((rows, w), d) for w, d in row_outs] + [
        jax.ShapeDtypeStruct((8, w), F32) for w in sums
    ]
    nbytes = sum(a.size * a.dtype.itemsize for a in list(row_ins) + stacks)
    return pl.pallas_call(
        kernel,
        grid_spec=pltpu.PrefetchScalarGridSpec(
            num_scalar_prefetch=1,
            grid=(rows // tile,),
            in_specs=in_specs,
            out_specs=out_specs,
            scratch_shapes=scratch,
        ),
        out_shape=out_shape,
        compiler_params=pltpu.CompilerParams(vmem_limit_bytes=56 * MIB, dimension_semantics=("arbitrary",)),
        cost_estimate=pl.CostEstimate(flops=flops, bytes_accessed=nbytes, transcendentals=0),
        name=name,
    )(meta, *row_ins, *vec_ins, *stacks)


def qkv_body(meta, rows, vecs, whole, outs, sums):
    (x,) = rows
    (bias,) = vecs
    width = whole[0].shape[1]
    for c in range(0, width, 1024):
        outs[0][:, c : c + 1024] = (nn(x[...], whole[0][:, c : c + 1024]) + bias[:, c : c + 1024]).astype(BF)


def out_body(meta, rows, vecs, whole, outs, sums):
    mixed, x = rows
    bias, gain, shift = vecs
    total = x[...].astype(F32) + (nn(mixed[...], whole[0][...]) + bias[...])
    centre = total - jnp.mean(total, axis=-1, keepdims=True)
    inverse = lax.rsqrt(jnp.mean(centre * centre, axis=-1, keepdims=True) + EPS)
    normed = centre * inverse
    outs[0][...] = normed
    outs[1][...] = jnp.broadcast_to(inverse, outs[1].shape)
    outs[2][...] = (normed * gain[...] + shift[...]).astype(BF)


def up_body(meta, rows, vecs, whole, outs, sums):
    (low,) = rows
    (bias,) = vecs
    width = whole[0].shape[1]
    step = 512
    for c in range(0, width, step):
        cols = slice(c, c + step)
        hidden = nn(low[...], whole[0][:, cols]) + bias[:, cols]
        cdf = 0.5 + 0.5 * lax.erf(hidden * 0.7071067811865476)
        pdf = jnp.exp(-0.5 * hidden * hidden) * 0.3989422804014327
        outs[0][:, cols] = (hidden * cdf).astype(BF)
        outs[1][:, cols] = (cdf + hidden * pdf).astype(BF)


def down_body(blk, per, meta, rows, vecs, whole, outs, sums):
    active, normed_one, cot = rows
    bias, gain_one, shift_one, gain, shift = vecs
    total = (normed_one[...] * gain_one[...] + shift_one[...]) + (nn(active[...], whole[0][...]) + bias[...])
    centre = total - jnp.mean(total, axis=-1, keepdims=True)
    inverse = lax.rsqrt(jnp.mean(centre * centre, axis=-1, keepdims=True) + EPS)
    normed = centre * inverse
    place = meta[2 + pl.program_id(0)]
    at = lax.broadcasted_iota(jnp.int32, (total.shape[0], 1), 0)
    valid = jnp.zeros(at.shape, jnp.bool_)
    for s in range(per):
        here = at - s * blk
        valid = valid | ((here >= 0) & (here < blk) & (here + place < meta[2 + pl.num_programs(0) + s]))
    keep = jnp.where(valid, 1.0, 0.0)
    outs[0][...] = ((normed * gain[...] + shift[...]) * keep).astype(BF)
    grad = cot[...].astype(F32) * keep
    sums[0][...] += fold(grad * normed)
    sums[1][...] += fold(grad)
    scaled = grad * gain[...]
    back = inverse * (
        scaled
        - jnp.mean(scaled, axis=-1, keepdims=True)
        - normed * jnp.mean(scaled * normed, axis=-1, keepdims=True)
    )
    low = back.astype(BF)
    outs[1][...] = back
    outs[2][...] = low
    sums[2][...] += fold(low.astype(F32))


def hidden_body(meta, rows, vecs, whole, outs, sums):
    second, deriv = rows
    width = deriv.shape[1]
    step = 512
    for c in range(0, width, step):
        cols = slice(c, c + step)
        low = (nt(second[...], whole[0][cols, :]) * deriv[:, cols].astype(F32)).astype(BF)
        outs[0][:, cols] = low
        sums[0][:, cols] += fold(low.astype(F32))


def first_body(meta, rows, vecs, whole, outs, sums):
    hidden, sum_two, normed, inverse = rows
    (gain,) = vecs
    grad = sum_two[...] + nt(hidden[...], whole[0][...])
    n1 = normed[...]
    sums[0][...] += fold(grad * n1)
    sums[1][...] += fold(grad)
    scaled = grad * gain[...]
    back = inverse[:, 0:1] * (
        scaled - jnp.mean(scaled, axis=-1, keepdims=True) - n1 * jnp.mean(scaled * n1, axis=-1, keepdims=True)
    )
    low = back.astype(BF)
    outs[0][...] = back
    outs[1][...] = low
    sums[2][...] += fold(low.astype(F32))
    outs[2][...] = nt(low, whole[1][...]).astype(BF)


def input_body(meta, rows, vecs, whole, outs, sums):
    proj, sum_one = rows
    width = sum_one.shape[1]
    total = sum_one[...]
    for c in range(3):
        total = total + nt(proj[c], whole[0][:, c * width : (c + 1) * width])
    outs[0][...] = total.astype(BF)


def key_mask(meta, n, blk):
    s = pl.program_id(0)
    length = meta[2 + n + s]
    at = lax.broadcasted_iota(jnp.int32, (n * blk, 1), 0)
    ok = jnp.zeros(at.shape, jnp.bool_)
    for j in range(n):
        here = at - j * blk
        ok = ok | ((here >= 0) & (here < blk) & (here + meta[2 + j] < length))
    return ok


def attend_kernel(n, blk, meta, q_ref, k_ref, v_ref, mixed_ref, lse_ref):
    ok = key_mask(meta, n, blk)
    q2 = q_ref[...].reshape(n * blk, 2 * HD) * BF(HD ** (-0.5))
    k2 = k_ref[...].reshape(n * blk, 2 * HD)
    v2 = v_ref[...].reshape(n * blk, 2 * HD)
    outs = []
    for h in range(2):
        lanes = slice(h * HD, (h + 1) * HD)
        scores = jnp.where(ok, nt(k2[:, lanes], q2[:, lanes]), NEG)
        peak = jnp.max(scores, axis=0, keepdims=True)
        weights = jnp.exp(scores - peak)
        total = jnp.sum(weights, axis=0, keepdims=True)
        probs = (weights * (1.0 / total)).astype(BF)
        lse_ref[h : h + 1, :] = peak + jnp.log(total)
        outs.append(tn(probs, v2[:, lanes]))
    mixed_ref[...] = jnp.concatenate(outs, axis=1).astype(BF).reshape(mixed_ref.shape)


def attend_back_kernel(n, blk, meta, q_ref, k_ref, v_ref, g_ref, lse_ref, proj_ref, sum_ref):
    ok = key_mask(meta, n, blk)
    scale = HD ** (-0.5)
    q2 = q_ref[...].reshape(n * blk, 2 * HD) * BF(scale)
    k2 = k_ref[...].reshape(n * blk, 2 * HD)
    v2 = v_ref[...].reshape(n * blk, 2 * HD)
    g2 = g_ref[...].reshape(n * blk, 2 * HD)
    gq, gk, gv = [], [], []
    for h in range(2):
        lanes = slice(h * HD, (h + 1) * HD)
        q, k, v, g = q2[:, lanes], k2[:, lanes], v2[:, lanes], g2[:, lanes]
        scores = jnp.where(ok, nt(k, q), NEG)
        exact = jnp.exp(scores - lse_ref[h : h + 1, :])
        mixed = exact * nt(v, g)
        inner = jnp.sum(mixed, axis=0, keepdims=True)
        low = (mixed - exact * inner).astype(BF)
        gq.append(tn(low, k) * scale)
        gk.append(nn(low, q))
        gv.append(nn(exact.astype(BF), g))
    for c, parts in enumerate((gq, gk, gv)):
        whole = jnp.concatenate(parts, axis=1).astype(BF)
        proj_ref[c] = whole.reshape(proj_ref.shape[1:])
        sum_ref[c] = fold(whole.astype(F32))


def attend(meta, proj, n, per, blk):
    heads = proj.shape[-1] // 3 // (2 * HD)
    shaped = proj.reshape(n, per, blk, proj.shape[-1])

    def spec(c):
        return pl.BlockSpec((n, None, blk, 2 * HD), lambda s, h, *_: (0, s, 0, c * heads + h))

    flops = per * heads * 2 * 4 * (n * blk) ** 2 * HD
    mixed, lse = pl.pallas_call(
        functools.partial(attend_kernel, n, blk),
        grid_spec=pltpu.PrefetchScalarGridSpec(
            num_scalar_prefetch=1,
            grid=(per, heads),
            in_specs=[spec(0), spec(1), spec(2)],
            out_specs=[spec(0), pl.BlockSpec((None, None, 2, n * blk), lambda s, h, *_: (s, h, 0, 0))],
        ),
        out_shape=[
            jax.ShapeDtypeStruct((n, per, blk, heads * 2 * HD), BF),
            jax.ShapeDtypeStruct((per, heads, 2, n * blk), F32),
        ],
        compiler_params=pltpu.CompilerParams(vmem_limit_bytes=48 * MIB),
        cost_estimate=pl.CostEstimate(flops=4 * flops, bytes_accessed=proj.size * 2, transcendentals=0),
        name="attend",
    )(meta, shaped, shaped, shaped)
    return mixed.reshape(n * per * blk, -1), lse


def attend_back(meta, proj, grad, lse, n, per, blk):
    width = proj.shape[-1] // 3
    heads = width // (2 * HD)
    shaped = proj.reshape(n, per, blk, proj.shape[-1])

    def spec(c):
        return pl.BlockSpec((n, None, blk, 2 * HD), lambda s, h, *_: (0, s, 0, c * heads + h))

    flops = per * heads * 2 * 10 * (n * blk) ** 2 * HD
    out, sums = pl.pallas_call(
        functools.partial(attend_back_kernel, n, blk),
        grid_spec=pltpu.PrefetchScalarGridSpec(
            num_scalar_prefetch=1,
            grid=(per, heads),
            in_specs=[spec(0), spec(1), spec(2), spec(0), pl.BlockSpec((None, None, 2, n * blk), lambda s, h, *_: (s, h, 0, 0))],
            out_specs=[
                pl.BlockSpec((3, n, None, blk, 2 * HD), lambda s, h, *_: (0, 0, s, 0, h)),
                pl.BlockSpec((3, None, 8, 2 * HD), lambda s, h, *_: (0, s, 0, h)),
            ],
        ),
        out_shape=[
            jax.ShapeDtypeStruct((3, n, per, blk, width), BF),
            jax.ShapeDtypeStruct((3, per, 8, width), F32),
        ],
        compiler_params=pltpu.CompilerParams(vmem_limit_bytes=48 * MIB),
        cost_estimate=pl.CostEstimate(flops=4 * flops, bytes_accessed=proj.size * 4, transcendentals=0),
        name="attend_back",
    )(meta, shaped, shaped, shaped, grad.reshape(n, per, blk, width), lse)
    return out.reshape(3, n * per * blk, width), sums


def contract_rows(left, right):
    return tn(left, right).astype(BF)


def shards(
    tokens, lengths, w_qkv, bias_qv, w_out, bias_out, gain_one, shift_one,
    w_up, bias_up, w_down, bias_down, gain_two, shift_two, cotangent,
):
    seqs, blk, width = tokens.shape
    n = lax.axis_size("ctx")
    ndp = lax.axis_size("dp")
    me = lax.axis_index("dp")
    place = lax.axis_index("ctx")
    per = seqs // n
    rows = seqs * blk
    tile = per * blk

    own = lax.dynamic_slice_in_dim(lengths, place * per, per)
    meta = jnp.concatenate(
        [
            jnp.stack([me, place]).astype(jnp.int32),
            (place ^ jnp.arange(n, dtype=jnp.int32)) * blk,
            own,
        ]
    )

    vectors = (bias_qv, bias_out, gain_one, shift_one, bias_up, bias_down, gain_two, shift_two)
    sizes = [v.shape[0] for v in vectors]
    packed = lax.all_gather(jnp.concatenate(vectors).reshape(1, -1), "dp", axis=0, tiled=True).astype(F32)
    fulls, pos = [], 0
    for size in sizes:
        fulls.append(packed[:, pos : pos + size].reshape(1, ndp * size))
        pos += size
    bqv, bout, gone, sone, bup, bdown, gtwo, stwo = fulls
    bqkv = jnp.concatenate([bqv[:, :width], jnp.zeros((1, width), F32), bqv[:, width:]], axis=1)

    x = to_sequences(tokens, None).reshape(rows, width)
    qkv_w = gather_dp(w_qkv)
    out_w = gather_dp(w_out)
    up_w = gather_dp(w_up)
    down_w = gather_dp(w_down)
    cot = to_sequences(cotangent, None).reshape(rows, width)

    ff = w_up.shape[1]
    flops = 2 * rows * width
    (proj,) = dense(qkv_body, "qkv", meta, rows, tile, [x], [bqkv], [qkv_w], [(3 * width, BF)], [], flops * 3 * width)
    mixed, lse = attend(meta, proj, n, per, blk)
    normed_one, inverse_one, first_low = dense(
        out_body, "out", meta, rows, tile, [mixed, x], [bout, gone, sone], [out_w],
        [(width, F32), (128, F32), (width, BF)], [], flops * width,
    )
    active, deriv = dense(up_body, "up", meta, rows, tile, [first_low], [bup], [up_w], [(ff, BF), (ff, BF)], [], flops * ff)
    out_parts, sum_two, second, s_gtwo, s_stwo, s_bdown = dense(
        functools.partial(down_body, blk, per), "down", meta, rows, tile, [active, normed_one, cot], [bdown, gone, sone, gtwo, stwo], [down_w],
        [(width, BF), (width, F32), (width, BF)], [width] * 3, flops * ff,
    )
    output = from_sequences(out_parts.reshape(n, per, blk, width), BF)
    grad_down = contract_rows(active, second)
    share_down = reduce_dp(grad_down)
    hidden, s_bup = dense(hidden_body, "hidden", meta, rows, tile, [second, deriv], [], [down_w], [(ff, BF)], [ff], flops * ff)
    grad_up = contract_rows(first_low, hidden)
    share_up = reduce_dp(grad_up)
    sum_one, branch, g_mixed, s_gone, s_sone, s_bout = dense(
        first_body, "first", meta, rows, tile, [hidden, sum_two, normed_one, inverse_one], [gone], [up_w, out_w],
        [(width, F32), (width, BF), (width, BF)], [width] * 3, flops * (ff + width),
    )
    grad_out = contract_rows(mixed, branch)
    share_out = reduce_dp(grad_out)
    g_proj, s_proj = attend_back(meta, proj, g_mixed, lse, n, per, blk)
    (grad_in,) = dense(input_body, "input", meta, rows, tile, [g_proj, sum_one], [], [qkv_w], [(width, BF)], [], flops * 3 * width)
    grad_input = from_sequences(grad_in.reshape(n, per, blk, width), F32)
    grad_qkv = jnp.concatenate([contract_rows(x, g_proj[c]) for c in range(3)], axis=1)
    share_qkv = reduce_dp(grad_qkv)

    s_proj = jnp.sum(s_proj, axis=(1, 2))
    vec = [jnp.concatenate([s_proj[0], s_proj[2]])] + [
        jnp.sum(s, axis=0) for s in (s_bout, s_gone, s_sone, s_bup, s_bdown, s_gtwo, s_stwo)
    ]
    vec = jnp.concatenate([v.reshape(ndp, -1) for v in vec], axis=1)
    vec = lax.psum(lax.psum_scatter(vec, "dp", scatter_dimension=0, tiled=True), "ctx").reshape(-1)
    grads, pos = [], 0
    for size in sizes:
        grads.append(vec[pos : pos + size])
        pos += size
    g_bqv, g_bout, g_gone, g_sone, g_bup, g_bdown, g_gtwo, g_stwo = grads
    return (
        output, grad_input, sum_ctx(share_qkv), g_bqv, sum_ctx(share_out), g_bout, g_gone, g_sone,
        sum_ctx(share_up), g_bup, sum_ctx(share_down), g_bdown, g_gtwo, g_stwo,
    )


def solution(mesh):
    row = P("dp", "ctx", None)
    mat = P("dp", None)
    vec = P("dp")
    weights = (mat, vec, mat, vec, vec, vec, mat, vec, mat, vec, vec, vec)
    return jax.shard_map(
        shards, mesh=mesh, in_specs=(row, vec) + weights + (row,), out_specs=(row, row) + weights, check_vma=False
    )
```

time: 1530 us -> 817 us (0.53)
  waiting for transfers between devices: 911 us -> 276 us
  matrix products: 286 us -> 39.6 us
  Pallas kernels: 0 us -> 187 us
  starting transfers between devices: 1.14 us -> 121 us
  local copies, waits for them, and re-layouts: 148 us -> 41.3 us
  blocking collectives: 107 us -> 82.3 us
    reduce_scatter x4 -> x0, waiting for transfers between devices: 357 us -> none  [the longest x1 118 us: shards(): lax.psum_scatter(grad_up, 'dp', scatter_dimension=0, tiled=True)]
    all_gather x6 -> x0, waiting for transfers between devices: 282 us -> none  [the longest x1 142 us: shards(): lax.all_gather(keys, 'ctx', axis=1, tiled=True)]
    ppermute x0 -> x64, waiting for transfers between devices: none -> 276 us  [the longest x52 208 us: swap(): return lax.ppermute(x, axis, [(i, i ^ bit) for i in range(n)])]
    dot_general x40 -> x6, matrix products: 286 us -> 39.6 us  [tn(): lax.dot_general(left, right, (((0,), (0,)), ((), ())), preferred_element_...]
    unnamed x15 -> x0, waiting for transfers between devices: 208 us -> none
    pallas_call x0 -> x9, Pallas kernels: none -> 187 us  [the longest x7 122 us: dense(): pl.pallas_call(kernel, grid_spec=pltpu.PrefetchScalarGridSpec(num_scalar_...]
    ppermute x0 -> x64, starting transfers between devices: none -> 121 us  [the longest x52 77.7 us: swap(): return lax.ppermute(x, axis, [(i, i ^ bit) for i in range(n)])]
    unnamed x109 -> x126, local copies, waits for them, and re-layouts: 103 us -> 19 us
  transfers between devices with their start and end apart: 13 -> 64, of which waited for: 12 -> 28; matrix products, arithmetic and copies ran while one was open for 18% -> 12% of each run, Pallas kernels for 0% -> 10%
where the time goes in v1:
time: 817 us; the launch traced here: 812 us
  waiting for transfers between devices  276 us (34%)
  Pallas kernels  187 us (23%)
  starting transfers between devices  121 us (15%)
  blocking collectives  82.3 us (10%)
  other arithmetic  62.6 us (8%)
  local copies, waits for them, and re-layouts  41.3 us (5%)
  matrix products  39.6 us (5%)
    ppermute x52, waiting for transfers between devices, swap(): return lax.ppermute(x, axis, [(i, i ^ bit) for i in range(n)])  208 us
    pallas_call x7, Pallas kernels, dense(): pl.pallas_call(kernel, grid_spec=pltpu.PrefetchScalarGridSpec(num_scalar_...  122 us
    ppermute x52, starting transfers between devices, swap(): return lax.ppermute(x, axis, [(i, i ^ bit) for i in range(n)])  77.7 us
    ppermute x4, waiting for transfers between devices, sum_ctx(): outer = lax.ppermute(total, 'ctx', [(1, 0), (2, 3)])  43.5 us
    all_gather x1, blocking collectives, shards(): lax.all_gather(jnp.concatenate(vectors).reshape(1, -1), 'dp', axis=0, til...  41.2 us
    pallas_call x1, Pallas kernels, attend_back(): pl.pallas_call(functools.partial(attend_back_kernel, n, blk), grid_spec=p...  40.2 us
    dot_general x6, matrix products, tn(): lax.dot_general(left, right, (((0,), (0,)), ((), ())), preferred_element_...  39.6 us
    ppermute x4, starting transfers between devices, sum_ctx(): inner = add_low(share, lax.ppermute(share, 'ctx', [(0, 1), (3, 2)]))  32.7 us
  transfers between devices with their start and end apart: 64, of which 28 were waited for; matrix products, arithmetic and copies ran while one was open for 12% of the time, Pallas kernels for 10%

profile of v1, /device:TPU:0, one launch (start us, length us, event | category | flops | bytes accessed | tf_op | source)
XLA Modules:
  0.0 812.4 jit_solution(18423645873976873757)
XLA Ops:
  7.7 14.6 %collective-permute-done.3 = bf16[128,3072]{1,0:T(8,128)(2,1)} collective-permute-done((bf16[128,3072]{1,0:T(8,128)(2,1)}, bf16[128,3072]{1,0:T(8,128)(2,1)}, u32[]{:S(2)}, u32[]{:S(2)}) %collective-permute-start.3) | collective-permute-done | bytes 786464 | tf_op jit(solution)/shard_map/ppermute | solution.py:21
  31.1 41.2 %all-gather.1 = bf16[8,1,1536]{2,1,0:T(2,128)(2,1)S(1)} all-gather(bf16[1,1,1536]{2,1,0:T(2,128)(2,1)S(1)} %reshape.208), channel_id=2, replica_groups=mesh['dp'=8,'ctx'=4] {'dp'}, dimensions={0}, use_global_device_ids=true | all-gather | bytes 27648 | tf_op jit(solution)/shard_map/all_gather | solution.py:446
  139.3 14.0 %collective-permute-start.18 = (bf16[2,128,1024]{2,1,0:T(8,128)(2,1)S(1)}, bf16[2,128,1024]{2,1,0:T(8,128)(2,1)S(1)}, u32[]{:S(2)}, u32[]{:S(2)}) collective-permute-start(bf16[2,128,1024]{2,1,0:T(8,128)(2,1)S(1)} %get-tuple-element.130), channel_id=1, source_target_pairs={{0,1},{1,0},{2,3},{3,2},{4,5},{5,4},{6,7},{7,6},{8,9},{9,8},{10,11... | collective-permute-start | bytes 1572872 | tf_op jit(solution)/shard_map/ppermute | solution.py:21
  170.5 27.7 %collective-permute-done.19 = bf16[2,128,1024]{2,1,0:T(8,128)(2,1)S(1)} collective-permute-done((bf16[2,128,1024]{2,1,0:T(8,128)(2,1)S(1)}, bf16[2,128,1024]{2,1,0:T(8,128)(2,1)S(1)}, u32[]{:S(2)}, u32[]{:S(2)}) %collective-permute-start.19) | collective-permute-done | bytes 524320 | tf_op jit(solution)/shard_map/ppermute | solution.py:21
  199.8 13.2 %qkv.1 = bf16[1024,3072]{1,0:T(8,128)(2,1)} custom-call(s32[8]{0:T(128)} %pad_add_fusion.meta_ref.meta, bf16[1024,1024]{1,0:T(8,128)(2,1)} %bitcast.234, f32[1,3072]{1,0:T(1,128)} %pad_maximum_fusion.19.refs_1_, bf16[4,128,3072]{2,1,0:T(8,128)(2,1)} %copy-done.6, bf16[4,128,3072]{2,1,0:T(8,128)(2,1)} %collective-permute-done.7.refs_3_), custom_call_target="tpu_custom_call" | custom-call | flops 6442450944 | bytes 8388608 | tf_op jit(solution)/shard_map/qkv/pallas_call | solution.py:188
  213.0 24.5 %attend.1 = (bf16[4,2,128,1024]{3,2,1,0:T(8,128)(2,1)S(1)}, f32[2,8,2,512]{3,2,1,0:T(2,128)S(1)}) custom-call(s32[8]{0:T(128)S(1)} %copy-done, bf16[4,2,128,3072]{3,2,1,0:T(8,128)(2,1)} %bitcast.278, bf16[4,2,128,3072]{3,2,1,0:T(8,128)(2,1)} %bitcast.279, bf16[4,2,128,3072]{3,2,1,0:T(8,128)(2,1)} %bitcast.280), custom_call_target="tpu_custom_call" | custom-call | flops 8589934592 | bytes 6291456 | tf_op jit(solution)/shard_map/attend/pallas_call | solution.py:368
  248.6 23.0 %up.1 = (bf16[1024,4096]{1,0:T(8,128)(2,1)}, bf16[1024,4096]{1,0:T(8,128)(2,1)}) custom-call(s32[8]{0:T(128)} %pad_add_fusion.meta_ref.meta, bf16[1024,1024]{1,0:T(8,128)(2,1)} %get-tuple-element.38.refs_0_, f32[1,4096]{1,0:T(1,128)} %bitcast.266, bf16[4,128,4096]{2,1,0:T(8,128)(2,1)} %pad_maximum_fusion.1.refs_2_.refs_5_, ...), custom_call_target="tpu_custom_call" | custom-call | flops 8589934592 | bytes 10485760 | tf_op jit(solution)/shard_map/up/pallas_call | solution.py:188
  271.6 21.4 %down.1 = (bf16[1024,1024]{1,0:T(8,128)(2,1)}, f32[1024,1024]{1,0:T(8,128)}, bf16[1024,1024]{1,0:T(8,128)(2,1)}, f32[8,1024]{1,0:T(8,128)}, f32[8,1024]{1,0:T(8,128)}, /*index=5*/f32[8,1024]{1,0:T(8,128)}) custom-call(s32[8]{0:T(128)} %pad_add_fusion.meta_ref.meta, bf16[1024,4096]{1,0:T(8,128)(2,1)} %get-tuple-element.39.refs_0_, ...), custom_call_target="tpu_custom_call" | custom-call | flops 8589934592 | bytes 23068672 | tf_op jit(solution)/shard_map/down/pallas_call | solution.py:188
  293.0 15.0 %convolution_convert_fusion = bf16[4096,1024]{0,1:T(8,128)(2,1)} fusion(bf16[1024,4096]{1,0:T(8,128)(2,1)} %get-tuple-element.39.refs_0_, bf16[1024,1024]{1,0:T(8,128)(2,1)} %get-tuple-element.42.refs_0_), kind=kOutput, calls=%fused_computation | convolution fusion | flops 8594128896 | bytes 18874368 | tf_op jit(solution)/shard_map/dot_general | solution.py:119
  307.9 18.0 %hidden.1 = (bf16[1024,4096]{1,0:T(8,128)(2,1)}, f32[8,4096]{1,0:T(8,128)}) custom-call(s32[8]{0:T(128)} %pad_add_fusion.meta_ref.meta, bf16[1024,1024]{1,0:T(8,128)(2,1)} %get-tuple-element.42.refs_0_, bf16[1024,4096]{1,0:T(8,128)(2,1)} %get-tuple-element.43.refs_1_, bf16[4,512,1024]{2,1,0:T(8,128)(2,1)} %pad_maximum_fusion.2.refs_8_.refs_2_, ...), custom_call_target="tpu_custom_call" | custom-call | flops 8589934592 | bytes 18874368 | tf_op jit(solution)/shard_map/hidden/pallas_call | solution.py:188
  326.0 15.0 %convolution_convert_fusion.1 = bf16[1024,4096]{1,0:T(8,128)(2,1)} fusion(bf16[1024,1024]{1,0:T(8,128)(2,1)S(1)} %copy-done.41, bf16[1024,4096]{1,0:T(8,128)(2,1)} %get-tuple-element.44.refs_0_), kind=kOutput, calls=%fused_computation.1 | convolution fusion | flops 8594128896 | bytes 18874368 | tf_op jit(solution)/shard_map/dot_general | solution.py:119
  341.0 22.9 %first.1 = (f32[1024,1024]{1,0:T(8,128)}, bf16[1024,1024]{1,0:T(8,128)(2,1)}, bf16[1024,1024]{1,0:T(8,128)(2,1)}, f32[8,1024]{1,0:T(8,128)}, f32[8,1024]{1,0:T(8,128)}, /*index=5*/f32[8,1024]{1,0:T(8,128)}) custom-call(s32[8]{0:T(128)} %pad_add_fusion.meta_ref.meta, bf16[1024,4096]{1,0:T(8,128)(2,1)} %get-tuple-element.44.refs_0_, ...), custom_call_target="tpu_custom_call" | custom-call | flops 10737418240 | bytes 27787264 | tf_op jit(solution)/shard_map/first/pallas_call | solution.py:188
  365.6 40.2 %attend_back.1 = (bf16[3,4,2,128,1024]{4,3,2,1,0:T(8,128)(2,1)}, f32[3,2,8,1024]{3,2,1,0:T(8,128)S(1)}) custom-call(s32[8]{0:T(128)S(1)} %copy-done.1, bf16[4,2,128,3072]{3,2,1,0:T(8,128)(2,1)} %bitcast.281, bf16[4,2,128,3072]{3,2,1,0:T(8,128)(2,1)} %bitcast.282, bf16[4,2,128,3072]{3,2,1,0:T(8,128)(2,1)} %bitcast.283, ...), custom_call_target="tpu_custom_call" | custom-call | flops 21474836480 | bytes 12582912 | tf_op jit(solution)/shard_map/attend_back/pallas_call | solution.py:396
  406.2 24.2 %all-reduce = f32[8,1536]{1,0:T(8,128)S(1)} all-reduce(f32[8,1536]{1,0:T(8,128)S(1)} %constant_dynamic-update-slice_fusion), channel_id=3, replica_groups=mesh['dp'=8,'ctx'=4] {'dp'}, use_global_device_ids=true, to_apply=%region_8.0.clone | all-reduce | flops 12288 | bytes 98304
  431.1 16.9 %psum.7 = f32[1,1536]{1,0:T(1,128)S(1)} all-reduce(f32[1,1536]{1,0:T(1,128)S(1)} %constant_dynamic-slice_fusion.6), channel_id=1, replica_groups=mesh['dp'=8,'ctx'=4] {'ctx'}, use_global_device_ids=true, to_apply=%region_9.0 | all-reduce | flops 1536 | bytes 12288 | tf_op jit(solution)/shard_map/psum | solution.py:497
  488.2 13.6 %input.1 = bf16[1024,1024]{1,0:T(8,128)(2,1)} custom-call(s32[8]{0:T(128)} %pad_add_fusion.meta_ref.meta, bf16[3,1024,1024]{2,1,0:T(8,128)(2,1)} %bitcast.228, f32[1024,1024]{1,0:T(8,128)} %get-tuple-element.50.refs_1_, bf16[4,128,3072]{2,1,0:T(8,128)(2,1)} %copy-done.6, bf16[4,128,3072]{2,1,0:T(8,128)(2,1)} %collective-permute-done.7.refs_3_), custom_call_target="tpu_custom_call" | custom-call | flops 6442450944 | bytes 16777216 | tf_op jit(solution)/shard_map/input/pallas_call | solution.py:188
  519.2 23.4 %collective-permute-done.30 = bf16[2,128,1024]{2,1,0:T(8,128)(2,1)S(1)} collective-permute-done((bf16[2,128,1024]{2,1,0:T(8,128)(2,1)S(1)}, bf16[2,128,1024]{2,1,0:T(8,128)(2,1)S(1)}, u32[]{:S(2)}, u32[]{:S(2)}) %collective-permute-start.30) | collective-permute-done | bytes 524320 | tf_op jit(solution)/shard_map/ppermute | solution.py:21
  582.8 22.6 %collective-permute-done.27 = bf16[2,128,1024]{2,1,0:T(8,128)(2,1)S(1)} collective-permute-done((bf16[2,128,1024]{2,1,0:T(8,128)(2,1)S(1)}, bf16[2,128,1024]{2,1,0:T(8,128)(2,1)S(1)}, u32[]{:S(2)}, u32[]{:S(2)}) %collective-permute-start.27) | collective-permute-done | bytes 524320 | tf_op jit(solution)/shard_map/ppermute | solution.py:21
  629.9 19.2 %collective-permute-done.57 = bf16[512,512]{0,1:T(8,128)(2,1)S(1)} collective-permute-done((bf16[512,512]{0,1:T(8,128)(2,1)S(1)}, bf16[512,512]{0,1:T(8,128)(2,1)S(1)}, u32[]{:S(2)}, u32[]{:S(2)}) %collective-permute-start.57) | collective-permute-done | bytes 524320 | tf_op jit(solution)/shard_map/ppermute | solution.py:21
  649.8 14.0 %collective-permute-done.49 = bf16[128,2048]{1,0:T(8,128)(2,1)S(1)} collective-permute-done((bf16[128,2048]{1,0:T(8,128)(2,1)S(1)}, bf16[128,2048]{1,0:T(8,128)(2,1)S(1)}, u32[]{:S(2)}, u32[]{:S(2)}) %collective-permute-start.49) | collective-permute-done | bytes 524320 | tf_op jit(solution)/shard_map/ppermute | solution.py:21
  670.3 19.6 %collective-permute-done.58 = bf16[512,1024]{0,1:T(8,128)(2,1)S(1)} collective-permute-done((bf16[512,1024]{0,1:T(8,128)(2,1)S(1)}, bf16[512,1024]{0,1:T(8,128)(2,1)S(1)}, u32[]{:S(2)}, u32[]{:S(2)}) %collective-permute-start.58) | collective-permute-done | bytes 1048608 | tf_op jit(solution)/shard_map/ppermute | solution.py:21
  721.8 15.7 %collective-permute-done.61 = bf16[512,1024]{0,1:T(8,128)(2,1)S(1)} collective-permute-done((bf16[512,1024]{0,1:T(8,128)(2,1)S(1)}, bf16[512,1024]{0,1:T(8,128)(2,1)S(1)}, u32[]{:S(2)}, u32[]{:S(2)}) %collective-permute-start.61) | collective-permute-done | bytes 1048608 | tf_op jit(solution)/shard_map/ppermute | solution.py:81
  760.9 14.6 %collective-permute-done.39 = bf16[128,3072]{0,1:T(8,128)(2,1)S(1)} collective-permute-done((bf16[128,3072]{0,1:T(8,128)(2,1)S(1)}, bf16[128,3072]{0,1:T(8,128)(2,1)S(1)}, u32[]{:S(2)}, u32[]{:S(2)}) %collective-permute-start.39) | collective-permute-done | bytes 786464 | tf_op jit(solution)/shard_map/ppermute | solution.py:83
  777.2 17.7 %collective-permute-done.63 = bf16[512,1024]{0,1:T(8,128)(2,1)} collective-permute-done((bf16[512,1024]{0,1:T(8,128)(2,1)S(1)}, bf16[512,1024]{0,1:T(8,128)(2,1)}, u32[]{:S(2)}, u32[]{:S(2)}) %collective-permute-start.63) | collective-permute-done | bytes 1048608 | tf_op jit(solution)/shard_map/ppermute | solution.py:83
  (369 shorter events, 317.4 us)
Async XLA Ops:
  3.6 73.8 %collective-permute-start.13 = (bf16[128,4096]{1,0:T(8,128)(2,1)}, bf16[128,4096]{1,0:T(8,128)(2,1)S(1)}, u32[]{:S(2)}, u32[]{:S(2)}) collective-permute-start(bf16[128,4096]{1,0:T(8,128)(2,1)} %param.23), channel_id=1, source_target_pairs={{0,8},{4,12},{8,0},{12,4},{16,24},{20,28},{24,16},{28,20},{1,9},{5... | collective-permute-start | bytes 3145736 | tf_op jit(solution)/shard_map/ppermute | solution.py:21
  3.7 70.4 %collective-permute-start.4 = (bf16[128,3072]{1,0:T(8,128)(2,1)}, bf16[128,3072]{1,0:T(8,128)(2,1)}, u32[]{:S(2)}, u32[]{:S(2)}) collective-permute-start(bf16[128,3072]{1,0:T(8,128)(2,1)} %param.17), channel_id=1, source_target_pairs={{0,16},{4,20},{8,24},{12,28},{16,0},{20,4},{24,8},{28,12},{1,17},{... | collective-permute-start | bytes 2359304 | tf_op jit(solution)/shard_map/ppermute | solution.py:21
  5.7 75.3 %collective-permute-start.14 = (bf16[128,4096]{1,0:T(8,128)(2,1)}, bf16[128,4096]{1,0:T(8,128)(2,1)}, u32[]{:S(2)}, u32[]{:S(2)}) collective-permute-start(bf16[128,4096]{1,0:T(8,128)(2,1)} %param.23), channel_id=1, source_target_pairs={{0,16},{4,20},{8,24},{12,28},{16,0},{20,4},{24,8},{28,12},{1,17},{... | collective-permute-start | bytes 3145736 | tf_op jit(solution)/shard_map/ppermute | solution.py:21
  5.8 77.9 %collective-permute-start.21 = (bf16[512,1024]{1,0:T(8,128)(2,1)}, bf16[512,1024]{1,0:T(8,128)(2,1)S(1)}, u32[]{:S(2)}, u32[]{:S(2)}) collective-permute-start(bf16[512,1024]{1,0:T(8,128)(2,1)} %param.25), channel_id=1, source_target_pairs={{0,8},{4,12},{8,0},{12,4},{16,24},{20,28},{24,16},{28,20},{1,9},{5... | collective-permute-start | bytes 3145736 | tf_op jit(solution)/shard_map/ppermute | solution.py:21
  22.3 62.0 %collective-permute-start.22 = (bf16[512,1024]{1,0:T(8,128)(2,1)}, bf16[512,1024]{1,0:T(8,128)(2,1)S(1)}, u32[]{:S(2)}, u32[]{:S(2)}) collective-permute-start(bf16[512,1024]{1,0:T(8,128)(2,1)} %param.25), channel_id=1, source_target_pairs={{0,16},{4,20},{8,24},{12,28},{16,0},{20,4},{24,8},{28,12},{1,17},{... | collective-permute-start | bytes 3145736 | tf_op jit(solution)/shard_map/ppermute | solution.py:21
  106.5 93.3 %collective-permute-start.7 = (bf16[4,128,3072]{2,1,0:T(8,128)(2,1)S(1)}, bf16[4,128,3072]{2,1,0:T(8,128)(2,1)}, u32[]{:S(2)}, u32[]{:S(2)}) collective-permute-start(bf16[4,128,3072]{2,1,0:T(8,128)(2,1)S(1)} %pad_maximum_fusion.5.refs_2_), channel_id=1, source_target_pairs={{0,4},{4,0},{8,12},{12,8},{16,20},{20,16},{24,28},{28,24},{1,5},{5... | collective-permute-start | bytes 9437192 | tf_op jit(solution)/shard_map/ppermute | solution.py:21
  110.1 138.5 %collective-permute-start.17 = (bf16[4,128,4096]{2,1,0:T(8,128)(2,1)}, bf16[4,128,4096]{2,1,0:T(8,128)(2,1)}, u32[]{:S(2)}, u32[]{:S(2)}) collective-permute-start(bf16[4,128,4096]{2,1,0:T(8,128)(2,1)} %pad_maximum_fusion.1.refs_2_.refs_5_), channel_id=1, source_target_pairs={{0,4},{4,0},{8,12},{12,8},{16,20},{20,16},{24,28},{28,24},{1,5},{5... | collective-permute-start | bytes 12582920 | tf_op jit(solution)/shard_map/ppermute | solution.py:21
  127.4 144.1 %collective-permute-start.25 = (bf16[4,512,1024]{2,1,0:T(8,128)(2,1)}, bf16[4,512,1024]{2,1,0:T(8,128)(2,1)}, u32[]{:S(2)}, u32[]{:S(2)}) collective-permute-start(bf16[4,512,1024]{2,1,0:T(8,128)(2,1)} %pad_maximum_fusion.2.refs_8_.refs_2_), channel_id=1, source_target_pairs={{0,4},{4,0},{8,12},{12,8},{16,20},{20,16},{24,28},{28,24},{1,5},{5... | collective-permute-start | bytes 12582920 | tf_op jit(solution)/shard_map/ppermute | solution.py:21
  153.9 44.3 %collective-permute-start.19 = (bf16[2,128,1024]{2,1,0:T(8,128)(2,1)S(1)}, bf16[2,128,1024]{2,1,0:T(8,128)(2,1)S(1)}, u32[]{:S(2)}, u32[]{:S(2)}) collective-permute-start(bf16[2,128,1024]{2,1,0:T(8,128)(2,1)S(1)} %get-tuple-element.132), channel_id=1, source_target_pairs={{0,2},{1,3},{2,0},{3,1},{4,6},{5,7},{6,4},{7,5},{8,10},{9,11},{10,... | collective-permute-start | bytes 1572872 | tf_op jit(solution)/shard_map/ppermute | solution.py:21
  198.2 40.6 %collective-permute-start.12 = (bf16[4,128,1024]{2,1,0:T(8,128)(2,1)S(1)}, bf16[4,128,1024]{2,1,0:T(8,128)(2,1)}, u32[]{:S(2)}, u32[]{:S(2)}) collective-permute-start(bf16[4,128,1024]{2,1,0:T(8,128)(2,1)S(1)} %pad_maximum_fusion.9.refs_5_.refs_7_), channel_id=1, source_target_pairs={{0,4},{4,0},{8,12},{12,8},{16,20},{20,16},{24,28},{28,24},{1,5},{5... | collective-permute-start | bytes 3145736 | tf_op jit(solution)/shard_map/ppermute | solution.py:21
  454.3 165.9 %collective-permute-start.56 = (bf16[4,512,1024]{1,2,0:T(8,128)(2,1)}, bf16[4,512,1024]{1,2,0:T(8,128)(2,1)}, u32[]{:S(2)}, u32[]{:S(2)}) collective-permute-start(bf16[4,512,1024]{1,2,0:T(8,128)(2,1)} %pad_maximum_fusion.4), channel_id=1, source_target_pairs={{0,4},{4,0},{8,12},{12,8},{16,20},{20,16},{24,28},{28,24},{1,5},{5... | collective-permute-start | bytes 12582920 | tf_op jit(solution)/shard_map/ppermute | solution.py:21
  458.6 167.7 %collective-permute-start.48 = (bf16[4,128,4096]{2,1,0:T(8,128)(2,1)}, bf16[4,128,4096]{2,1,0:T(8,128)(2,1)}, u32[]{:S(2)}, u32[]{:S(2)}) collective-permute-start(bf16[4,128,4096]{2,1,0:T(8,128)(2,1)} %pad_maximum_fusion.3), channel_id=1, source_target_pairs={{0,4},{4,0},{8,12},{12,8},{16,20},{20,16},{24,28},{28,24},{1,5},{5... | collective-permute-start | bytes 12582920 | tf_op jit(solution)/shard_map/ppermute | solution.py:21
  464.0 53.7 %collective-permute-start.40 = (bf16[4,128,1024]{1,2,0:T(8,128)(2,1)}, bf16[4,128,1024]{1,2,0:T(8,128)(2,1)S(1)}, u32[]{:S(2)}, u32[]{:S(2)}) collective-permute-start(bf16[4,128,1024]{1,2,0:T(8,128)(2,1)} %pad_maximum_fusion.10), channel_id=1, source_target_pairs={{0,4},{4,0},{8,12},{12,8},{16,20},{20,16},{24,28},{28,24},{1,5},{5... | collective-permute-start | bytes 3145736 | tf_op jit(solution)/shard_map/ppermute | solution.py:21
  487.7 84.6 %collective-permute-start.32 = (bf16[4,128,3072]{1,2,0:T(8,128)(2,1)}, bf16[4,128,3072]{1,2,0:T(8,128)(2,1)}, u32[]{:S(2)}, u32[]{:S(2)}) collective-permute-start(bf16[4,128,3072]{1,2,0:T(8,128)(2,1)} %pad_maximum_fusion.6), channel_id=1, source_target_pairs={{0,4},{4,0},{8,12},{12,8},{16,20},{20,16},{24,28},{28,24},{1,5},{5... | collective-permute-start | bytes 9437192 | tf_op jit(solution)/shard_map/ppermute | solution.py:21
  562.0 43.4 %collective-permute-start.27 = (bf16[2,128,1024]{2,1,0:T(8,128)(2,1)S(1)}, bf16[2,128,1024]{2,1,0:T(8,128)(2,1)S(1)}, u32[]{:S(2)}, u32[]{:S(2)}) collective-permute-start(bf16[2,128,1024]{2,1,0:T(8,128)(2,1)S(1)} %bitcast.251), channel_id=1, source_target_pairs={{0,2},{1,3},{2,0},{3,1},{4,6},{5,7},{6,4},{7,5},{8,10},{9,11},{10,... | collective-permute-start | bytes 1572872 | tf_op jit(solution)/shard_map/ppermute | solution.py:21
  607.4 111.2 %collective-permute-start.46 = (bf16[128,1024]{0,1:T(8,128)(2,1)S(1)}, bf16[128,1024]{0,1:T(8,128)(2,1)S(1)}, u32[]{:S(2)}, u32[]{:S(2)}) collective-permute-start(bf16[128,1024]{0,1:T(8,128)(2,1)S(1)} %add_convert_fusion.16), channel_id=1, source_target_pairs={{1,2},{2,1},{5,6},{6,5},{9,10},{10,9},{13,14},{14,13},{17,18},{18,... | collective-permute-start | bytes 786440 | tf_op jit(solution)/shard_map/ppermute | solution.py:82
  614.0 52.6 %collective-permute-start.34 = (bf16[128,3072]{0,1:T(8,128)(2,1)S(1)}, bf16[128,3072]{0,1:T(8,128)(2,1)S(1)}, u32[]{:S(2)}, u32[]{:S(2)}) collective-permute-start(bf16[128,3072]{0,1:T(8,128)(2,1)S(1)} %pad_maximum_fusion.15), channel_id=1, source_target_pairs={{0,8},{4,12},{8,0},{12,4},{16,24},{20,28},{24,16},{28,20},{1,9},{5... | collective-permute-start | bytes 2359304 | tf_op jit(solution)/shard_map/ppermute | solution.py:21
  620.2 46.7 %collective-permute-start.36 = (bf16[128,3072]{0,1:T(8,128)(2,1)S(1)}, bf16[128,3072]{0,1:T(8,128)(2,1)}, u32[]{:S(2)}, u32[]{:S(2)}) collective-permute-start(bf16[128,3072]{0,1:T(8,128)(2,1)S(1)} %pad_maximum_fusion.16), channel_id=1, source_target_pairs={{0,16},{4,20},{8,24},{12,28},{16,0},{20,4},{24,8},{28,12},{1,17},{... | collective-permute-start | bytes 2359304 | tf_op jit(solution)/shard_map/ppermute | solution.py:21
  664.2 37.6 %collective-permute-start.60 = (bf16[512,1024]{0,1:T(8,128)(2,1)S(1)}, bf16[512,1024]{0,1:T(8,128)(2,1)S(1)}, u32[]{:S(2)}, u32[]{:S(2)}) collective-permute-start(bf16[512,1024]{0,1:T(8,128)(2,1)S(1)} %pad_maximum_fusion.14), channel_id=1, source_target_pairs={{0,16},{4,20},{8,24},{12,28},{16,0},{20,4},{24,8},{28,12},{1,17},{... | collective-permute-start | bytes 3145736 | tf_op jit(solution)/shard_map/ppermute | solution.py:21
  666.6 40.2 %collective-permute-start.50 = (bf16[128,4096]{1,0:T(8,128)(2,1)S(1)}, bf16[128,4096]{1,0:T(8,128)(2,1)S(1)}, u32[]{:S(2)}, u32[]{:S(2)}) collective-permute-start(bf16[128,4096]{1,0:T(8,128)(2,1)S(1)} %pad_maximum_fusion.11), channel_id=1, source_target_pairs={{0,8},{4,12},{8,0},{12,4},{16,24},{20,28},{24,16},{28,20},{1,9},{5... | collective-permute-start | bytes 3145736 | tf_op jit(solution)/shard_map/ppermute | solution.py:21
  666.9 39.9 %collective-permute-start.52 = (bf16[128,4096]{1,0:T(8,128)(2,1)S(1)}, bf16[128,4096]{1,0:T(8,128)(2,1)S(1)}, u32[]{:S(2)}, u32[]{:S(2)}) collective-permute-start(bf16[128,4096]{1,0:T(8,128)(2,1)S(1)} %pad_maximum_fusion.12), channel_id=1, source_target_pairs={{0,16},{4,20},{8,24},{12,28},{16,0},{20,4},{24,8},{28,12},{1,17},{... | collective-permute-start | bytes 3145736 | tf_op jit(solution)/shard_map/ppermute | solution.py:21
  708.7 40.0 %collective-permute-start.53 = (bf16[128,4096]{1,0:T(8,128)(2,1)S(1)}, bf16[128,4096]{1,0:T(8,128)(2,1)S(1)}, u32[]{:S(2)}, u32[]{:S(2)}) collective-permute-start(bf16[128,4096]{1,0:T(8,128)(2,1)S(1)} %add_convert_fusion.5), channel_id=1, source_target_pairs={{0,1},{3,2},{4,5},{7,6},{8,9},{11,10},{12,13},{15,14},{16,17},{19,... | collective-permute-start | bytes 3145736 | tf_op jit(solution)/shard_map/ppermute | solution.py:81
  755.9 39.1 %collective-permute-start.63 = (bf16[512,1024]{0,1:T(8,128)(2,1)S(1)}, bf16[512,1024]{0,1:T(8,128)(2,1)}, u32[]{:S(2)}, u32[]{:S(2)}) collective-permute-start(bf16[512,1024]{0,1:T(8,128)(2,1)S(1)} %add_convert_fusion), channel_id=1, source_target_pairs={{1,0},{2,3},{5,4},{6,7},{9,8},{10,11},{13,12},{14,15},{17,16},{18,... | collective-permute-start | bytes 3145736 | tf_op jit(solution)/shard_map/ppermute | solution.py:83
  759.6 49.7 %collective-permute-start.55 = (bf16[128,4096]{1,0:T(8,128)(2,1)}, bf16[128,4096]{1,0:T(8,128)(2,1)}, u32[]{:S(2)}, u32[]{:S(2)}) collective-permute-start(bf16[128,4096]{1,0:T(8,128)(2,1)} %add_convert_fusion.3), channel_id=1, source_target_pairs={{1,0},{2,3},{5,4},{6,7},{9,8},{10,11},{13,12},{14,15},{17,16},{18,... | collective-permute-start | bytes 3145736 | tf_op jit(solution)/shard_map/ppermute | solution.py:83
  (91 other events, 1648.4 us)

commit v2 on v1

--- a/solution.py
+++ b/solution.py
@@ -13,6 +13,13 @@
 BF = jnp.bfloat16
 F32 = jnp.float32
 MIB = 1024 * 1024
+COSTS = {'qkv': 13, 'out': 10, 'up': 23, 'down': 21, 'hidden': 18, 'first': 23, 'input': 14, 'attend': 24, 'attend_back': 21, 'gd_away': 11, 'gd_keep': 11, 'gu_away': 11, 'gu_keep': 11, 'gb_away': 10, 'gb_keep': 10, 'gc_away': 8, 'gc_keep': 8}
+
+
+def cost(name):
+    return pl.CostEstimate(flops=COSTS[name] * 1000000000, bytes_accessed=1000000, transcendentals=0)
+
+
 ANY = pl.BlockSpec(memory_space=pl.ANY)
 
 
@@ -21,22 +28,42 @@
     return lax.ppermute(x, axis, [(i, i ^ bit) for i in range(n)])
 
 
-def gather_dp(own):
-    n = lax.axis_size("dp")
-    if n == 8:
-        half = own.shape[1] // 2
-        at_x = swap(own, "dp", 2)
-        at_y = swap(own, "dp", 4)
-        left = swap(at_x[:, :half], "dp", 4)
-        right = swap(at_y[:, half:], "dp", 2)
-        mine = jnp.stack([own, at_x, at_y, jnp.concatenate([left, right], axis=1)])
-    else:
-        mine = own[None]
-        bit = 2
-        while bit < n:
-            mine = jnp.concatenate([mine, swap(mine, "dp", bit)])
-            bit *= 2
-    return mine, swap(mine, "dp", 1)
+def after(x, *others):
+    return lax.optimization_barrier((x,) + others)[0]
+
+
+def sync(*values):
+    return lax.optimization_barrier(values)
+
+
+def gather_near(own):
+    if lax.axis_size("dp") != 8:
+        return ()
+    return swap(own, "dp", 2), swap(own, "dp", 4)
+
+
+def gather_far(near):
+    if not near:
+        return ()
+    half = near[0].shape[1] // 2
+    return swap(near[0][:, :half], "dp", 4), swap(near[1][:, half:], "dp", 2)
+
+
+def gather_stack(own, near, far):
+    if near:
+        return jnp.stack([own, near[0], near[1], jnp.concatenate(far, axis=1)])
+    mine = own[None]
+    bit = 2
+    while bit < lax.axis_size("dp"):
+        mine = jnp.concatenate([mine, swap(mine, "dp", bit)])
+        bit *= 2
+    return mine
+
+
+def gather_direct(own):
+    if lax.axis_size("dp") != 8:
+        return (own,)
+    return (own,) + tuple(swap(own, "dp", bit) for bit in (2, 4, 6))
 
 
 def add_low(*parts):
@@ -46,26 +73,18 @@
     return total.astype(BF)
 
 
-def reduce_dp(grad):
+def reduce_any(grad):
     n = lax.axis_size("dp")
     me = lax.axis_index("dp")
     rows = grad.shape[0] // n
     width = grad.shape[1]
 
-    def shard(rel):
-        return lax.dynamic_slice(grad, ((me ^ rel) * rows, 0), (rows, width))
-
-    away = jnp.stack([shard(2 * k + 1) for k in range(n // 2)])
-    come = swap(away, "dp", 1)
-    if n == 8:
-        half = width // 2
-        own, to_x, to_y, to_xy = (add_low(shard(2 * k), come[k]) for k in range(4))
-        left = swap(to_xy[:, :half], "dp", 4)
-        right = swap(to_xy[:, half:], "dp", 2)
-        to_x = jnp.concatenate([add_low(to_x[:, :half], left), to_x[:, half:]], axis=1)
-        to_y = jnp.concatenate([to_y[:, :half], add_low(to_y[:, half:], right)], axis=1)
-        return add_low(own, swap(to_x, "dp", 2), swap(to_y, "dp", 4))
-    mine = add_low(jnp.stack([shard(2 * k) for k in range(n // 2)]), come)
+    def stack(odd):
+        return jnp.stack(
+            [lax.dynamic_slice(grad, ((me ^ (2 * k + odd)) * rows, 0), (rows, width)) for k in range(n // 2)]
+        )
+
+    mine = add_low(stack(0), swap(stack(1), "dp", 1))
     bit = n // 2
     while bit > 1:
         keep = mine.shape[0] // 2
@@ -74,37 +93,66 @@
     return mine[0]
 
 
+def send_far(sums):
+    return swap(sums[3], "dp", 4), swap(sums[4], "dp", 2)
+
+
+def send_near(sums, far):
+    own, to_x, to_y = sums[:3]
+    cut = far[0].shape[1]
+    to_x = jnp.concatenate([add_low(to_x[:, :cut], far[0]), to_x[:, cut:]], axis=1)
+    to_y = jnp.concatenate([to_y[:, :cut], add_low(to_y[:, cut:], far[1])], axis=1)
+    return swap(to_x, "dp", 2), swap(to_y, "dp", 4)
+
+
 def sum_ctx(share):
+    if lax.axis_size("ctx") != 4:
+        return lax.psum(share.astype(F32), "ctx").astype(BF)
+    inner = add_low(share, send_in(share))
+    total = add_low(inner, send_mid(inner))
+    return pick(total, send_out(total))
+
+
+def send_in(share):
+    return lax.ppermute(share, "ctx", [(0, 1), (3, 2)])
+
+
+def send_mid(inner):
+    return lax.ppermute(inner, "ctx", [(1, 2), (2, 1)])
+
+
+def send_out(total):
+    return lax.ppermute(total, "ctx", [(1, 0), (2, 3)])
+
+
+def pick(total, outer):
+    place = lax.axis_index("ctx")
+    return jnp.where((place == 0) | (place == 3), outer, total)
+
+
+def to_sequences(block):
     n = lax.axis_size("ctx")
-    if n != 4:
-        return lax.psum(share.astype(F32), "ctx")
-    inner = add_low(share, lax.ppermute(share, "ctx", [(0, 1), (3, 2)]))
-    total = add_low(inner, lax.ppermute(inner, "ctx", [(1, 2), (2, 1)]))
-    outer = lax.ppermute(total, "ctx", [(1, 0), (2, 3)])
-    place = lax.axis_index("ctx")
-    return jnp.where((place == 0) | (place == 3), outer, total).astype(F32)
-
-
-def to_sequences(block, order):
+    return lax.all_to_all(block.reshape((n, -1) + block.shape[1:]), "ctx", 0, 0, tiled=True)
+
+
+def part_of(block, j):
     n = lax.axis_size("ctx")
+    per = block.shape[0] // n
+    return lax.dynamic_slice_in_dim(block, (lax.axis_index("ctx") ^ j) * per, per, axis=0)
+
+
+def put_slots(pieces, dtype):
+    n = len(pieces)
     me = lax.axis_index("ctx")
-    per = block.shape[0] // n
-
-    def part(j):
-        return lax.dynamic_slice_in_dim(block, (me ^ j) * per, per, axis=0)
-
-    return jnp.stack([part(0)] + [swap(part(j), "ctx", j) for j in range(1, n)])
-
-
-def from_sequences(parts, dtype):
-    n = lax.axis_size("ctx")
-    me = lax.axis_index("ctx")
-    per = parts.shape[1]
-    out = jnp.zeros((n * per,) + parts.shape[2:], dtype)
+    per = pieces[0].shape[0]
+    out = jnp.zeros((n * per,) + pieces[0].shape[1:], dtype)
     for j in range(n):
-        piece = parts[j] if j == 0 else swap(parts[j], "ctx", j)
-        out = lax.dynamic_update_slice_in_dim(out, piece.astype(dtype), (me ^ j) * per, axis=0)
+        out = lax.dynamic_update_slice_in_dim(out, pieces[j].astype(dtype), (me ^ j) * per, axis=0)
     return out
+
+
+def trade(block, j):
+    return swap(block, "ctx", j)
 
 
 def nn(left, right):
@@ -123,15 +171,16 @@
     return jnp.sum(rows.reshape(rows.shape[0] // 8, 8, rows.shape[1]), axis=0)
 
 
-def fetch(stacks, whole, sems, me):
+def fetch(stacks, whole, sems, me, rows, first):
     copies = []
+    width = whole.shape[1]
     for odd, stack in enumerate(stacks):
-        count, rows, _ = stack.shape
+        count = stack.shape[0]
         for k in range(count):
             start = pl.multiple_of((me ^ (2 * k + odd)) * rows, rows)
             copies.append(
                 pltpu.make_async_copy(
-                    stack.at[k], whole.at[pl.ds(start, rows)], sems.at[odd * count + k]
+                    stack.at[k, pl.ds(0, rows), pl.ds(first, width)], whole.at[pl.ds(start, rows)], sems.at[odd * count + k]
                 )
             )
     for copy in copies:
@@ -148,11 +197,11 @@
     return pl.BlockSpec((height, width), lambda i, *_: (0, 0))
 
 
-def dense(body, name, meta, rows, tile, row_ins, vec_ins, weights, row_outs, sums, flops):
-    stacks = [s for pair in weights for s in pair]
+def dense(body, name, meta, rows, tile, row_ins, vec_ins, weights, row_outs, sums):
+    stacks = [s for w in weights for s in w[:2]]
     scratch = []
-    for mine, other in weights:
-        count, r, width = mine.shape
+    for mine, other, r, _, width in weights:
+        count = mine.shape[0]
         scratch.append(pltpu.VMEM((2 * count * r, width), BF))
         scratch.append(pltpu.SemaphoreType.DMA((2 * count,)))
     n_row, n_vec, n_stack = len(row_ins), len(vec_ins), len(stacks)
@@ -169,7 +218,7 @@
         @pl.when(pl.program_id(0) == 0)
         def _():
             for w in range(len(weights)):
-                fetch(stack_refs[2 * w : 2 * w + 2], scratch_refs[2 * w], scratch_refs[2 * w + 1], meta_ref[0])
+                fetch(stack_refs[2 * w : 2 * w + 2], scratch_refs[2 * w], scratch_refs[2 * w + 1], meta_ref[0], weights[w][2], weights[w][3])
             for ref in sum_refs:
                 ref[...] = jnp.zeros_like(ref)
 
@@ -184,7 +233,6 @@
     out_shape = [jax.ShapeDtypeStruct((rows, w), d) for w, d in row_outs] + [
         jax.ShapeDtypeStruct((8, w), F32) for w in sums
     ]
-    nbytes = sum(a.size * a.dtype.itemsize for a in list(row_ins) + stacks)
     return pl.pallas_call(
         kernel,
         grid_spec=pltpu.PrefetchScalarGridSpec(
@@ -196,7 +244,7 @@
         ),
         out_shape=out_shape,
         compiler_params=pltpu.CompilerParams(vmem_limit_bytes=56 * MIB, dimension_semantics=("arbitrary",)),
-        cost_estimate=pl.CostEstimate(flops=flops, bytes_accessed=nbytes, transcendentals=0),
+        cost_estimate=cost(name),
         name=name,
     )(meta, *row_ins, *vec_ins, *stacks)
 
@@ -295,11 +343,16 @@
 
 
 def input_body(meta, rows, vecs, whole, outs, sums):
-    proj, sum_one = rows
+    sum_one = rows[-1]
     width = sum_one.shape[1]
     total = sum_one[...]
-    for c in range(3):
-        total = total + nt(proj[c], whole[0][:, c * width : (c + 1) * width])
+    first = 0
+    for proj in rows[:-1]:
+        part = proj.shape[2]
+        for c in range(3):
+            start = c * width + first
+            total = total + nt(proj[c], whole[0][:, start : start + part])
+        first += part
     outs[0][...] = total.astype(BF)
 
 
@@ -364,7 +417,6 @@
     def spec(c):
         return pl.BlockSpec((n, None, blk, 2 * HD), lambda s, h, *_: (0, s, 0, c * heads + h))
 
-    flops = per * heads * 2 * 4 * (n * blk) ** 2 * HD
     mixed, lse = pl.pallas_call(
         functools.partial(attend_kernel, n, blk),
         grid_spec=pltpu.PrefetchScalarGridSpec(
@@ -378,45 +430,168 @@
             jax.ShapeDtypeStruct((per, heads, 2, n * blk), F32),
         ],
         compiler_params=pltpu.CompilerParams(vmem_limit_bytes=48 * MIB),
-        cost_estimate=pl.CostEstimate(flops=4 * flops, bytes_accessed=proj.size * 2, transcendentals=0),
+        cost_estimate=cost("attend"),
         name="attend",
     )(meta, shaped, shaped, shaped)
     return mixed.reshape(n * per * blk, -1), lse
 
 
-def attend_back(meta, proj, grad, lse, n, per, blk):
+def attend_back(meta, proj, grad, lse, n, per, blk, first, count):
     width = proj.shape[-1] // 3
     heads = width // (2 * HD)
     shaped = proj.reshape(n, per, blk, proj.shape[-1])
 
     def spec(c):
-        return pl.BlockSpec((n, None, blk, 2 * HD), lambda s, h, *_: (0, s, 0, c * heads + h))
-
-    flops = per * heads * 2 * 10 * (n * blk) ** 2 * HD
+        return pl.BlockSpec((n, None, blk, 2 * HD), lambda s, h, *_: (0, s, 0, c * heads + first + h))
+
     out, sums = pl.pallas_call(
         functools.partial(attend_back_kernel, n, blk),
         grid_spec=pltpu.PrefetchScalarGridSpec(
             num_scalar_prefetch=1,
-            grid=(per, heads),
-            in_specs=[spec(0), spec(1), spec(2), spec(0), pl.BlockSpec((None, None, 2, n * blk), lambda s, h, *_: (s, h, 0, 0))],
+            grid=(per, count),
+            in_specs=[spec(0), spec(1), spec(2), spec(0), pl.BlockSpec((None, None, 2, n * blk), lambda s, h, *_: (s, first + h, 0, 0))],
             out_specs=[
                 pl.BlockSpec((3, n, None, blk, 2 * HD), lambda s, h, *_: (0, 0, s, 0, h)),
                 pl.BlockSpec((3, None, 8, 2 * HD), lambda s, h, *_: (0, s, 0, h)),
             ],
         ),
         out_shape=[
-            jax.ShapeDtypeStruct((3, n, per, blk, width), BF),
-            jax.ShapeDtypeStruct((3, per, 8, width), F32),
+            jax.ShapeDtypeStruct((3, n, per, blk, count * 2 * HD), BF),
+            jax.ShapeDtypeStruct((3, per, 8, count * 2 * HD), F32),
         ],
         compiler_params=pltpu.CompilerParams(vmem_limit_bytes=48 * MIB),
-        cost_estimate=pl.CostEstimate(flops=4 * flops, bytes_accessed=proj.size * 4, transcendentals=0),
+        cost_estimate=cost("attend_back"),
         name="attend_back",
     )(meta, shaped, shaped, shaped, grad.reshape(n, per, blk, width), lse)
-    return out.reshape(3, n * per * blk, width), sums
-
-
-def contract_rows(left, right):
-    return tn(left, right).astype(BF)
+    return out.reshape(3, n * per * blk, count * 2 * HD), sums
+
+
+def weight_grad(name, meta, odd, lefts, rights, chunk, come=None, extra=None):
+    rows = lefts[0].shape[0]
+    tall = lefts[0].shape[1] // 8
+    plan = []
+    for li, group in enumerate(rights):
+        for right in group:
+            for c in range((right.shape[0] if right.ndim == 3 else 1) * (right.shape[-1] // chunk)):
+                plan.append((li, right, c))
+    steps = len(plan)
+    flat = [r for group in rights for r in group]
+    firsts, pos = [], 0
+    for right in flat:
+        firsts.append(pos)
+        pos += (right.shape[0] if right.ndim == 3 else 1) * (right.shape[-1] // chunk)
+    owners = [li for li, group in enumerate(rights) for _ in group]
+    below = 0 if extra is None else extra.shape[1]
+    cut = (steps + 1) // 2
+    n_left = len(lefts)
+
+    def kernel(meta_ref, *refs):
+        left_refs = refs[: 4 * n_left]
+        pos = 4 * n_left
+        right_refs = refs[pos : pos + len(flat)]
+        pos += len(flat)
+        extra_refs = refs[pos : pos + 4] if below else ()
+        pos += len(extra_refs)
+        come_ref = refs[pos] if come is not None else None
+        pos += come is not None
+        outs = refs[pos:-1]
+        turned = refs[-1]
+        c = pl.program_id(0)
+
+        @pl.when(c == 0)
+        def _():
+            for i in range(4 * n_left):
+                turned[i * tall : (i + 1) * tall, :] = left_refs[i][...].T
+
+        def store(total):
+            for k in range(4):
+                part = total[k * tall : (k + 1) * tall]
+                if come is None:
+                    outs[0][k, 0:tall, :] = part.astype(BF)
+                    if below:
+                        outs[0][k, tall:, :] = extra_refs[k][...]
+                    continue
+                part = (part + come_ref[k, 0:tall, :].astype(F32)).astype(BF)
+                if below:
+                    low = (extra_refs[k][...].astype(F32) + come_ref[k, tall:, :].astype(F32)).astype(BF)
+                if k < 3:
+                    outs[k][0:tall, :] = part
+                    if below:
+                        outs[k][tall:, :] = low
+                    continue
+
+                @pl.when(c < cut)
+                def _():
+                    outs[3][0:tall, :] = part
+                    if below:
+                        outs[3][tall:, :] = low
+
+                @pl.when(c >= cut)
+                def _():
+                    outs[4][0:tall, :] = part
+                    if below:
+                        outs[4][tall:, :] = low
+
+        for i, right_ref in enumerate(right_refs):
+            last = firsts[i + 1] if i + 1 < len(flat) else steps
+            li = owners[i]
+
+            @pl.when((c >= firsts[i]) & (c < last))
+            def _(right_ref=right_ref, li=li):
+                store(nn(turned[4 * li * tall : 4 * (li + 1) * tall, :], right_ref[...]))
+
+    def left_spec(k):
+        return pl.BlockSpec((rows, tall), lambda c, m: (0, m[0] ^ (2 * k + odd)))
+
+    def right_spec(i, right):
+        last = (firsts[i + 1] if i + 1 < len(flat) else steps) - 1
+        inner = right.shape[-1] // chunk
+
+        def place(c):
+            return jnp.clip(c, firsts[i], last) - firsts[i]
+
+        if right.ndim == 3:
+            return pl.BlockSpec((None, rows, chunk), lambda c, m: (place(c) // inner, 0, place(c) % inner))
+        return pl.BlockSpec((rows, chunk), lambda c, m: (0, place(c)))
+
+    def extra_spec(k):
+        return pl.BlockSpec((None, below, chunk), lambda c, m: (m[0] ^ (2 * k + odd), 0, c))
+
+    high = tall + below
+    four = pl.BlockSpec((4, high, chunk), lambda c, m: (0, 0, c))
+    in_specs = [left_spec(k) for _ in lefts for k in range(4)] + [right_spec(i, r) for i, r in enumerate(flat)]
+    args = [left for left in lefts for _ in range(4)] + flat
+    if below:
+        in_specs += [extra_spec(k) for k in range(4)]
+        args += [extra] * 4
+    if come is None:
+        out_specs = [four]
+        out_shape = [jax.ShapeDtypeStruct((4, high, steps * chunk), BF)]
+    else:
+        in_specs.append(four)
+        args.append(come)
+        out_specs = [pl.BlockSpec((high, chunk), lambda c, m: (0, c))] * 3 + [
+            pl.BlockSpec((high, chunk), lambda c, m: (0, jnp.minimum(c, cut - 1))),
+            pl.BlockSpec((high, chunk), lambda c, m: (0, jnp.maximum(c - cut, 0))),
+        ]
+        out_shape = [jax.ShapeDtypeStruct((high, steps * chunk), BF)] * 3 + [
+            jax.ShapeDtypeStruct((high, cut * chunk), BF),
+            jax.ShapeDtypeStruct((high, (steps - cut) * chunk), BF),
+        ]
+    return pl.pallas_call(
+        kernel,
+        grid_spec=pltpu.PrefetchScalarGridSpec(
+            num_scalar_prefetch=1,
+            grid=(steps,),
+            in_specs=in_specs,
+            out_specs=out_specs,
+            scratch_shapes=[pltpu.VMEM((4 * n_left * tall, rows), BF)],
+        ),
+        out_shape=out_shape,
+        compiler_params=pltpu.CompilerParams(vmem_limit_bytes=56 * MIB),
+        cost_estimate=cost(name),
+        name=name,
+    )(meta, *args)
 
 
 def shards(
@@ -431,19 +606,34 @@
     per = seqs // n
     rows = seqs * blk
     tile = per * blk
+    ff = w_up.shape[1]
+    thin = w_qkv.shape[0]
+    tuned = ndp == 8
+    half = width // (2 * HD) // 2
 
     own = lax.dynamic_slice_in_dim(lengths, place * per, per)
     meta = jnp.concatenate(
-        [
-            jnp.stack([me, place]).astype(jnp.int32),
-            (place ^ jnp.arange(n, dtype=jnp.int32)) * blk,
-            own,
-        ]
+        [jnp.stack([me, place]).astype(jnp.int32), jnp.arange(n, dtype=jnp.int32) * blk, own]
     )
 
     vectors = (bias_qv, bias_out, gain_one, shift_one, bias_up, bias_down, gain_two, shift_two)
     sizes = [v.shape[0] for v in vectors]
-    packed = lax.all_gather(jnp.concatenate(vectors).reshape(1, -1), "dp", axis=0, tiled=True).astype(F32)
+    count = sum(sizes)
+    line = jnp.pad(jnp.concatenate(vectors).reshape(1, count), ((0, 15), (0, 3 * width - count)))
+    qkv_own = jnp.concatenate([w_qkv, line])
+    qkv_parts = gather_direct(qkv_own)
+    mid_own = jnp.concatenate([w_out, w_up], axis=1)
+    mid_near = gather_near(mid_own)
+    x = to_sequences(tokens).reshape(rows, width)
+    x, qkv_parts, mid_near, cotangent = sync(x, qkv_parts, mid_near, cotangent)
+    qkv_mine = jnp.stack(qkv_parts) if tuned else gather_stack(qkv_parts[0], (), ())
+    qkv_other = swap(qkv_mine, "dp", 1)
+    mid_far = gather_far(mid_near)
+    cot_1 = trade(part_of(cotangent, 1), 1)
+
+    both = jnp.concatenate([qkv_mine[:, thin, :count], qkv_other[:, thin, :count]])
+    index = jnp.arange(ndp, dtype=jnp.int32) ^ me
+    packed = jnp.take(both, (index >> 1) + (index & 1) * (ndp // 2), axis=0).astype(F32)
     fulls, pos = [], 0
     for size in sizes:
         fulls.append(packed[:, pos : pos + size].reshape(1, ndp * size))
@@ -451,58 +641,166 @@
     bqv, bout, gone, sone, bup, bdown, gtwo, stwo = fulls
     bqkv = jnp.concatenate([bqv[:, :width], jnp.zeros((1, width), F32), bqv[:, width:]], axis=1)
 
-    x = to_sequences(tokens, None).reshape(rows, width)
-    qkv_w = gather_dp(w_qkv)
-    out_w = gather_dp(w_out)
-    up_w = gather_dp(w_up)
-    down_w = gather_dp(w_down)
-    cot = to_sequences(cotangent, None).reshape(rows, width)
-
-    ff = w_up.shape[1]
-    flops = 2 * rows * width
-    (proj,) = dense(qkv_body, "qkv", meta, rows, tile, [x], [bqkv], [qkv_w], [(3 * width, BF)], [], flops * 3 * width)
+    qkv_w = (qkv_mine, qkv_other, thin, 0, 3 * width)
+    (proj,) = dense(qkv_body, "qkv", meta, rows, tile, [x], [bqkv], [qkv_w], [(3 * width, BF)], [])
+    proj, mid_far, cot_1, w_down, cotangent = sync(proj, mid_far, cot_1, w_down, cotangent)
+    mid_mine = gather_stack(mid_own, mid_near, mid_far)
+    mid_other = swap(mid_mine, "dp", 1)
+    down_near = gather_near(w_down)
+    cot_2 = trade(part_of(cotangent, 2), 2)
     mixed, lse = attend(meta, proj, n, per, blk)
+    mixed, mid_other, down_near, cot_2 = sync(mixed, mid_other, down_near, cot_2)
+    out_w = (mid_mine, mid_other, thin, 0, width)
+    up_w = (mid_mine, mid_other, thin, width, ff)
+    down_far = gather_far(down_near)
     normed_one, inverse_one, first_low = dense(
-        out_body, "out", meta, rows, tile, [mixed, x], [bout, gone, sone], [out_w],
-        [(width, F32), (128, F32), (width, BF)], [], flops * width,
+        out_body, "out", meta, rows, tile, [mixed, x], [bout, gone, sone], [out_w], [(width, F32), (128, F32), (width, BF)], []
     )
-    active, deriv = dense(up_body, "up", meta, rows, tile, [first_low], [bup], [up_w], [(ff, BF), (ff, BF)], [], flops * ff)
+    first_low, down_far, cotangent = sync(first_low, down_far, cotangent)
+    down_mine = gather_stack(w_down, down_near, down_far)
+    down_other = swap(down_mine, "dp", 1)
+    cot_3 = trade(part_of(cotangent, 3), 3)
+    active, deriv = dense(up_body, "up", meta, rows, tile, [first_low], [bup], [up_w], [(ff, BF), (ff, BF)], [])
+    active, down_other, cot_3 = sync(active, down_other, cot_3)
+    down_w = (down_mine, down_other, w_down.shape[0], 0, width)
+    cot = put_slots([part_of(cotangent, 0), cot_1, cot_2, cot_3], BF).reshape(rows, width)
     out_parts, sum_two, second, s_gtwo, s_stwo, s_bdown = dense(
-        functools.partial(down_body, blk, per), "down", meta, rows, tile, [active, normed_one, cot], [bdown, gone, sone, gtwo, stwo], [down_w],
-        [(width, BF), (width, F32), (width, BF)], [width] * 3, flops * ff,
+        functools.partial(down_body, blk, per), "down", meta, rows, tile, [active, normed_one, cot],
+        [bdown, gone, sone, gtwo, stwo], [down_w], [(width, BF), (width, F32), (width, BF)], [width] * 3,
     )
-    output = from_sequences(out_parts.reshape(n, per, blk, width), BF)
-    grad_down = contract_rows(active, second)
-    share_down = reduce_dp(grad_down)
-    hidden, s_bup = dense(hidden_body, "hidden", meta, rows, tile, [second, deriv], [], [down_w], [(ff, BF)], [ff], flops * ff)
-    grad_up = contract_rows(first_low, hidden)
-    share_up = reduce_dp(grad_up)
+    out_parts = out_parts.reshape(n * per, blk, width)
+    out_own = part_of(out_parts, 0)
+    out_2 = trade(part_of(out_parts, 2), 2)
+
+    come = ()
+    if tuned:
+        (away,) = weight_grad("gd_away", meta, 1, [active], [[second]], 256)
+        come = swap(away, "dp", 1)
+        second = after(second, away)
+    hidden, s_bup = dense(hidden_body, "hidden", meta, rows, tile, [second, deriv], [], [down_w], [(ff, BF)], [ff])
+    hidden, come, out_2, out_parts = sync(hidden, come, out_2, out_parts)
+    out_1 = trade(part_of(out_parts, 1), 1)
+    d_far, d_near = (), ()
+    if tuned:
+        d_sums = weight_grad("gd_keep", meta, 0, [active], [[second]], 256, come=come)
+        d_far = send_far(d_sums)
+        (away,) = weight_grad("gu_away", meta, 1, [first_low], [[after(hidden, d_sums[0])]], 512)
+        hidden = after(hidden, away)
+        away, d_far, out_1 = sync(away, d_far, out_1)
+        come = swap(away, "dp", 1)
+    hidden, d_far, out_1, out_parts = sync(hidden, d_far, out_1, out_parts)
+    if tuned:
+        d_near = send_near(d_sums, d_far)
+    out_3 = trade(part_of(out_parts, 3), 3)
     sum_one, branch, g_mixed, s_gone, s_sone, s_bout = dense(
         first_body, "first", meta, rows, tile, [hidden, sum_two, normed_one, inverse_one], [gone], [up_w, out_w],
-        [(width, F32), (width, BF), (width, BF)], [width] * 3, flops * (ff + width),
+        [(width, F32), (width, BF), (width, BF)], [width] * 3,
     )
-    grad_out = contract_rows(mixed, branch)
-    share_out = reduce_dp(grad_out)
-    g_proj, s_proj = attend_back(meta, proj, g_mixed, lse, n, per, blk)
-    (grad_in,) = dense(input_body, "input", meta, rows, tile, [g_proj, sum_one], [], [qkv_w], [(width, BF)], [], flops * 3 * width)
-    grad_input = from_sequences(grad_in.reshape(n, per, blk, width), F32)
-    grad_qkv = jnp.concatenate([contract_rows(x, g_proj[c]) for c in range(3)], axis=1)
-    share_qkv = reduce_dp(grad_qkv)
-
-    s_proj = jnp.sum(s_proj, axis=(1, 2))
+    branch, g_mixed, come, d_near, out_3 = sync(branch, g_mixed, come, d_near, out_3)
+    output = put_slots([out_own, out_1, out_2, out_3], BF)
+    d_in, u_far = (), ()
+    if tuned:
+        d_share = add_low(d_sums[0], *d_near)
+        d_in = send_in(d_share)
+        u_sums = weight_grad("gu_keep", meta, 0, [first_low], [[hidden]], 512, come=come)
+        u_far = send_far(u_sums)
+        g_mixed = after(g_mixed, u_sums[0])
+    p_one, s_one = attend_back(meta, proj, g_mixed, lse, n, per, blk, 0, half)
+    p_one, d_in, u_far = sync(p_one, d_in, u_far)
+    d_mid, u_near = (), ()
+    if tuned:
+        u_near = send_near(u_sums, u_far)
+        d_inner = add_low(d_share, d_in)
+        d_mid = send_mid(d_inner)
+        (away,) = weight_grad("gb_away", meta, 1, [x, mixed], [[p_one], [branch]], 256)
+        come = swap(away, "dp", 1)
+        g_mixed = after(g_mixed, away)
+    p_two, s_two = attend_back(meta, proj, g_mixed, lse, n, per, blk, half, half)
+    p_two, come, u_near, d_mid = sync(p_two, come, u_near, d_mid)
+
+    s_proj = jnp.concatenate([jnp.sum(s_one, axis=(1, 2)), jnp.sum(s_two, axis=(1, 2))], axis=1)
     vec = [jnp.concatenate([s_proj[0], s_proj[2]])] + [
         jnp.sum(s, axis=0) for s in (s_bout, s_gone, s_sone, s_bup, s_bdown, s_gtwo, s_stwo)
     ]
     vec = jnp.concatenate([v.reshape(ndp, -1) for v in vec], axis=1)
-    vec = lax.psum(lax.psum_scatter(vec, "dp", scatter_dimension=0, tiled=True), "ctx").reshape(-1)
+
+    d_out, u_in, come_two = (), (), ()
+    if tuned:
+        d_total = add_low(d_inner, d_mid)
+        d_out = send_out(d_total)
+        u_share = add_low(u_sums[0], *u_near)
+        u_in = send_in(u_share)
+        extra = jnp.pad(vec[:, None, :].astype(BF), ((0, 0), (0, 15), (0, 3 * (width // 2) - count)))
+        (away,) = weight_grad("gc_away", meta, 1, [x], [[p_two]], 256, extra=extra)
+        come_two = swap(away, "dp", 1)
+        sum_one = after(sum_one, away)
+    (grad_in,) = dense(input_body, "input", meta, rows, tile, [p_one, p_two, sum_one], [], [qkv_w], [(width, BF)], [])
+    grad_in, d_out, u_in, come_two = sync(grad_in, d_out, u_in, come_two)
+    grad_in = grad_in.reshape(n * per, blk, width)
+    in_own = part_of(grad_in, 0)
+    in_2, in_3 = trade(part_of(grad_in, 2), 2), trade(part_of(grad_in, 3), 3)
+    if tuned:
+        u_inner = add_low(u_share, u_in)
+        u_mid = send_mid(u_inner)
+        b_sums = weight_grad("gb_keep", meta, 0, [x, mixed], [[p_one], [branch]], 256, come=after(come, grad_in))
+        b_sums, come_two, u_mid = sync(b_sums, come_two, u_mid)
+        b_far = send_far(b_sums)
+        c_sums = weight_grad("gc_keep", meta, 0, [x], [[p_two]], 256, come=come_two, extra=extra)
+        c_sums, b_far = sync(c_sums, b_far)
+        b_near = send_near(b_sums, b_far)
+        c_sums, b_near = sync(c_sums, b_near)
+        c_far = send_far(c_sums)
+        b_share = add_low(b_sums[0], *b_near)
+        b_in = send_in(b_share)
+        c_near = send_near(c_sums, c_far)
+        c_near, b_in, in_2, in_3, grad_in = sync(c_near, b_in, in_2, in_3, grad_in)
+    in_1 = trade(part_of(grad_in, 1), 1)
+    if tuned:
+        c_share = add_low(c_sums[0], *c_near)
+        c_in = send_in(c_share)
+        b_inner = add_low(b_share, b_in)
+        b_mid = send_mid(b_inner)
+        u_total = add_low(u_inner, u_mid)
+        u_out = send_out(u_total)
+        b_mid, c_in, u_out, in_1 = sync(b_mid, c_in, u_out, in_1)
+        b_total = add_low(b_inner, b_mid)
+        b_out = send_out(b_total)
+        c_inner = add_low(c_share, c_in)
+        c_total = add_low(c_inner, send_mid(c_inner))
+        d_total = pick(d_total, d_out)
+        u_total = pick(u_total, u_out)
+        b_total = pick(b_total, b_out)
+        c_total = pick(c_total, send_out(c_total)).astype(F32)
+        b_total = b_total.astype(F32)
+        part = width // 2
+        pieces = []
+        for c in range(3):
+            pieces += [b_total[:, c * part : (c + 1) * part], c_total[:thin, c * part : (c + 1) * part]]
+        g_qkv = jnp.concatenate(pieces, axis=1)
+        g_out = b_total[:, 3 * part :]
+        g_up = u_total.astype(F32)
+        g_down = d_total.astype(F32)
+        vec = c_total[thin, :count]
+    else:
+        def whole(*products):
+            return jnp.concatenate([tn(a, b).astype(BF) for a, b in products], axis=1)
+
+        def total(grad):
+            return sum_ctx(reduce_any(grad)).astype(F32)
+
+        g_down = total(whole((active, second)))
+        g_up = total(whole((first_low, hidden)))
+        g_out = total(whole((mixed, branch)))
+        g_qkv = total(whole(*[(x, p[c]) for c in range(3) for p in (p_one, p_two)]))
+        vec = lax.psum(lax.psum_scatter(vec, "dp", scatter_dimension=0, tiled=True), "ctx").reshape(-1)
     grads, pos = [], 0
     for size in sizes:
         grads.append(vec[pos : pos + size])
         pos += size
     g_bqv, g_bout, g_gone, g_sone, g_bup, g_bdown, g_gtwo, g_stwo = grads
+    grad_input = put_slots([in_own, in_1, in_2, in_3], F32)
     return (
-        output, grad_input, sum_ctx(share_qkv), g_bqv, sum_ctx(share_out), g_bout, g_gone, g_sone,
-        sum_ctx(share_up), g_bup, sum_ctx(share_down), g_bdown, g_gtwo, g_stwo,
+        output, grad_input, g_qkv, g_bqv, g_out, g_bout, g_gone, g_sone, g_up, g_bup, g_down, g_bdown, g_gtwo, g_stwo,
     )
 
 

time: 817 us -> 610 us (0.75)
  waiting for transfers between devices: 276 us -> 139 us
  Pallas kernels: 187 us -> 274 us
  blocking collectives: 82.3 us -> 0 us
  matrix products: 39.6 us -> 0 us
  starting transfers between devices: 121 us -> 96 us
  other arithmetic: 62.6 us -> 42.8 us
    ppermute x52 -> x43, waiting for transfers between devices: 208 us -> 87.2 us  [swap(): return lax.ppermute(x, axis, [(i, i ^ bit) for i in range(n)])]
    pallas_call x0 -> x8, Pallas kernels: none -> 85.9 us  [weight_grad(): pl.pallas_call(kernel, grid_spec=pltpu.PrefetchScalarGridSpec(num_scalar_...]
    all_gather x1 -> x0, blocking collectives: 41.2 us -> none  [shards(): lax.all_gather(jnp.concatenate(vectors).reshape(1, -1), 'dp', axis=0, til...]
    dot_general x6 -> x0, matrix products: 39.6 us -> none  [tn(): lax.dot_general(left, right, (((0,), (0,)), ((), ())), preferred_element_...]
    unnamed x1 -> x0, blocking collectives: 24.2 us -> none
    ppermute x12, starting transfers between devices: 43.6 us -> 22.4 us  [the longest x4 13.2 us: send_in(): return lax.ppermute(share, 'ctx', [(0, 1), (3, 2)])]
    ppermute x12, waiting for transfers between devices: 68.5 us -> 51.6 us  [the longest x4 39.6 us: send_out(): return lax.ppermute(total, 'ctx', [(1, 0), (2, 3)])]
    psum x1 -> x0, blocking collectives: 16.9 us -> none  [shards(): lax.psum(lax.psum_scatter(vec, 'dp', scatter_dimension=0, tiled=True), 'c...]
  transfers between devices with their start and end apart: 64 -> 56, of which waited for: 28 -> 16; matrix products, arithmetic and copies ran while one was open for 12% -> 10% of each run, Pallas kernels for 10% -> 35%
where the time goes in v2:
time: 610 us; the launch traced here: 600 us
  Pallas kernels  274 us (45%)
  waiting for transfers between devices  139 us (23%)
  starting transfers between devices  96 us (16%)
  local copies, waits for them, and re-layouts  45.4 us (7%)
  other arithmetic  42.8 us (7%)
    pallas_call x7, Pallas kernels, dense(): pl.pallas_call(kernel, grid_spec=pltpu.PrefetchScalarGridSpec(num_scalar_...  122 us
    ppermute x43, waiting for transfers between devices, swap(): return lax.ppermute(x, axis, [(i, i ^ bit) for i in range(n)])  87.2 us
    pallas_call x8, Pallas kernels, weight_grad(): pl.pallas_call(kernel, grid_spec=pltpu.PrefetchScalarGridSpec(num_scalar_...  85.9 us
    ppermute x43, starting transfers between devices, swap(): return lax.ppermute(x, axis, [(i, i ^ bit) for i in range(n)])  67.2 us
    pallas_call x2, Pallas kernels, attend_back(): pl.pallas_call(functools.partial(attend_back_kernel, n, blk), grid_spec=p...  41.6 us
    ppermute x4, waiting for transfers between devices, send_out(): return lax.ppermute(total, 'ctx', [(1, 0), (2, 3)])  39.6 us
    pallas_call x1, Pallas kernels, attend(): pl.pallas_call(functools.partial(attend_kernel, n, blk), grid_spec=pltpu....  24.5 us
    unnamed x156, local copies, waits for them, and re-layouts  16.3 us
  transfers between devices with their start and end apart: 56, of which 16 were waited for; matrix products, arithmetic and copies ran while one was open for 10% of the time, Pallas kernels for 35%

profile of v2, /device:TPU:0, one launch (start us, length us, event | category | flops | bytes accessed | tf_op | source)
XLA Modules:
  0.0 599.9 jit_solution(597492979676207431)
XLA Ops:
  19.3 40.5 %collective-permute-done = bf16[144,3072]{1,0:T(8,128)(2,1)S(1)} collective-permute-done((bf16[144,3072]{1,0:T(8,128)(2,1)}, bf16[144,3072]{1,0:T(8,128)(2,1)S(1)}, u32[]{:S(2)}, u32[]{:S(2)}) %collective-permute-start) | collective-permute-done | bytes 884768 | tf_op jit(solution)/shard_map/ppermute | solution.py:28
  59.9 18.7 %collective-permute-done.1 = bf16[144,3072]{1,0:T(8,128)(2,1)S(1)} collective-permute-done((bf16[144,3072]{1,0:T(8,128)(2,1)}, bf16[144,3072]{1,0:T(8,128)(2,1)S(1)}, u32[]{:S(2)}, u32[]{:S(2)}) %collective-permute-start.1) | collective-permute-done | bytes 884768 | tf_op jit(solution)/shard_map/ppermute | solution.py:28
  99.8 13.1 %qkv.1 = bf16[1024,3072]{1,0:T(8,128)(2,1)} custom-call(s32[8]{0:T(128)} %pad_add_fusion.meta_ref.meta, bf16[1024,1024]{1,0:T(8,128)(2,1)} %bitcast.106, f32[1,3072]{1,0:T(1,128)} %pad_maximum_fusion.12.refs_1_, bf16[4,144,3072]{2,1,0:T(8,128)(2,1)} %copy-done.10, bf16[4,144,3072]{2,1,0:T(8,128)(2,1)} %collective-permute-done.5.refs_3_.refs_4_), custom_call_target="tpu_custom_call" | custom-call | flops 12999999488 | bytes 1000000 | tf_op jit(solution)/shard_map/qkv/pallas_call | solution.py:236
  125.0 24.5 %attend.1 = (bf16[4,2,128,1024]{3,2,1,0:T(8,128)(2,1)S(1)}, f32[2,8,2,512]{3,2,1,0:T(2,128)S(1)}) custom-call(s32[8]{0:T(128)S(1)} %copy-done, bf16[4,2,128,3072]{3,2,1,0:T(8,128)(2,1)} %bitcast.156, bf16[4,2,128,3072]{3,2,1,0:T(8,128)(2,1)} %bitcast.157, bf16[4,2,128,3072]{3,2,1,0:T(8,128)(2,1)} %bitcast.158), custom_call_target="tpu_custom_call" | custom-call | flops 24000000000 | bytes 1000000 | tf_op jit(solution)/shard_map/attend/pallas_call | solution.py:420
  153.8 9.7 %out.1 = (f32[1024,1024]{1,0:T(8,128)}, f32[1024,128]{1,0:T(8,128)}, bf16[1024,1024]{1,0:T(8,128)(2,1)}) custom-call(s32[8]{0:T(128)} %pad_add_fusion.meta_ref.meta, bf16[1024,1024]{1,0:T(8,128)(2,1)} %bitcast.90, bf16[1024,1024]{1,0:T(8,128)(2,1)} %bitcast.107, f32[1,1024]{1,0:T(1,128)} %bitcast.153, f32[1,1024]{1,0:T(1,128)} %bitcast.145, ...), custom_call_target="tpu_custom_call" | custom-call | flops 10000000000 | bytes 1000000 | tf_op jit(solution)/shard_map/out/pallas_call | solution.py:236
  170.8 23.7 %up.1 = (bf16[1024,4096]{1,0:T(8,128)(2,1)}, bf16[1024,4096]{1,0:T(8,128)(2,1)}) custom-call(s32[8]{0:T(128)} %pad_add_fusion.meta_ref.meta, bf16[1024,1024]{1,0:T(8,128)(2,1)} %get-tuple-element.174.refs_0_.refs_1_.refs_2_.refs_3_, f32[1,4096]{1,0:T(1,128)} %bitcast.138, bf16[4,128,5120]{2,1,0:T(8,128)(2,1)} %pad_maximum_fusion.refs_5_.refs_2_.refs_7_, ...), custom_call_target="tpu_custom_call" | custom-call | flops 23000000512 | bytes 1000000 | tf_op jit(solution)/shard_map/up/pallas_call | solution.py:236
  197.0 21.1 %down.1 = (bf16[1024,1024]{1,0:T(8,128)(2,1)}, f32[1024,1024]{1,0:T(8,128)}, bf16[1024,1024]{1,0:T(8,128)(2,1)}, f32[8,1024]{1,0:T(8,128)}, f32[8,1024]{1,0:T(8,128)}, /*index=5*/f32[8,1024]{1,0:T(8,128)}) custom-call(s32[8]{0:T(128)} %pad_add_fusion.meta_ref.meta, bf16[1024,4096]{1,0:T(8,128)(2,1)} %get-tuple-element.179.refs_0_.refs_1_.refs_2_.refs_3_, ...), custom_call_target="tpu_custom_call" | custom-call | flops 20999999488 | bytes 1000000 | tf_op jit(solution)/shard_map/down/pallas_call | solution.py:236
  218.2 10.6 %gd_away.1 = bf16[4,512,1024]{2,1,0:T(8,128)(2,1)} custom-call(s32[8]{0:T(128)} %pad_add_fusion.meta_ref.meta, bf16[1024,4096]{1,0:T(8,128)(2,1)} %get-tuple-element.179.refs_0_.refs_1_.refs_2_.refs_3_, bf16[1024,4096]{1,0:T(8,128)(2,1)} %get-tuple-element.179.refs_0_.refs_1_.refs_2_.refs_3_, ...), custom_call_target="tpu_custom_call" | custom-call | flops 11000000512 | bytes 1000000 | tf_op jit(solution)/shard_map/gd_away/pallas_call | solution.py:581
  233.7 17.8 %hidden.1 = (bf16[1024,4096]{1,0:T(8,128)(2,1)}, f32[8,4096]{1,0:T(8,128)}) custom-call(s32[8]{0:T(128)} %pad_add_fusion.meta_ref.meta, bf16[1024,1024]{1,0:T(8,128)(2,1)} %get-tuple-element.187.refs_4_.refs_0_, bf16[1024,4096]{1,0:T(8,128)(2,1)} %get-tuple-element.188.refs_1_, bf16[4,512,1024]{2,1,0:T(8,128)(2,1)} %pad_maximum_fusion.1.refs_8_.refs_2_, ...), custom_call_target="tpu_custom_call" | custom-call | flops 17999998976 | bytes 1000000 | tf_op jit(solution)/shard_map/hidden/pallas_call | solution.py:236
  257.7 11.6 %gd_keep.1 = (bf16[512,1024]{1,0:T(8,128)(2,1)}, bf16[512,1024]{1,0:T(8,128)(2,1)}, bf16[512,1024]{1,0:T(8,128)(2,1)}, bf16[512,512]{1,0:T(8,128)(2,1)}, bf16[512,512]{1,0:T(8,128)(2,1)}) custom-call(s32[8]{0:T(128)} %pad_add_fusion.meta_ref.meta, bf16[1024,4096]{1,0:T(8,128)(2,1)} %get-tuple-element.179.refs_0_.refs_1_.refs_2_.refs_3_, ...), custom_call_target="tpu_custom_call" | custom-call | flops 11000000512 | bytes 1000000 | tf_op jit(solution)/shard_map/gd_keep/pallas_call | solution.py:581
  271.0 11.7 %gu_away.1 = bf16[4,128,4096]{2,1,0:T(8,128)(2,1)} custom-call(s32[8]{0:T(128)} %pad_add_fusion.meta_ref.meta, bf16[1024,1024]{1,0:T(8,128)(2,1)} %get-tuple-element.174.refs_0_.refs_1_.refs_2_.refs_3_, bf16[1024,1024]{1,0:T(8,128)(2,1)} %get-tuple-element.174.refs_0_.refs_1_.refs_2_.refs_3_, ...), custom_call_target="tpu_custom_call" | custom-call | flops 11000000512 | bytes 1000000 | tf_op jit(solution)/shard_map/gu_away/pallas_call | solution.py:581
  295.7 22.9 %first.1 = (f32[1024,1024]{1,0:T(8,128)}, bf16[1024,1024]{1,0:T(8,128)(2,1)}, bf16[1024,1024]{1,0:T(8,128)(2,1)}, f32[8,1024]{1,0:T(8,128)}, f32[8,1024]{1,0:T(8,128)}, /*index=5*/f32[8,1024]{1,0:T(8,128)}) custom-call(s32[8]{0:T(128)} %pad_add_fusion.meta_ref.meta, bf16[1024,4096]{1,0:T(8,128)(2,1)} %get-tuple-element.203.refs_4_.refs_0_, ...), custom_call_target="tpu_custom_call" | custom-call | flops 23000000512 | bytes 1000000 | tf_op jit(solution)/shard_map/first/pallas_call | solution.py:236
  326.7 12.5 %gu_keep.1 = (bf16[128,4096]{1,0:T(8,128)(2,1)}, bf16[128,4096]{1,0:T(8,128)(2,1)}, bf16[128,4096]{1,0:T(8,128)(2,1)}, bf16[128,2048]{1,0:T(8,128)(2,1)}, bf16[128,2048]{1,0:T(8,128)(2,1)}) custom-call(s32[8]{0:T(128)} %pad_add_fusion.meta_ref.meta, bf16[1024,1024]{1,0:T(8,128)(2,1)} %get-tuple-element.174.refs_0_.refs_1_.refs_2_.refs_3_, ...), custom_call_target="tpu_custom_call" | custom-call | flops 11000000512 | bytes 1000000 | tf_op jit(solution)/shard_map/gu_keep/pallas_call | solution.py:581
  340.7 20.8 %attend_back.2 = (bf16[3,4,2,128,512]{4,3,2,1,0:T(8,128)(2,1)S(1)}, f32[3,2,8,512]{3,2,1,0:T(8,128)S(1)}) custom-call(s32[8]{0:T(128)S(1)} %copy-done.1, bf16[4,2,128,3072]{3,2,1,0:T(8,128)(2,1)} %bitcast.159, bf16[4,2,128,3072]{3,2,1,0:T(8,128)(2,1)} %bitcast.160, bf16[4,2,128,3072]{3,2,1,0:T(8,128)(2,1)} %bitcast.161, ...), custom_call_target="tpu_custom_call" | custom-call | flops 20999999488 | bytes 1000000 | tf_op jit(solution)/shard_map/attend_back/pallas_call | solution.py:447
  365.1 11.6 %gb_away.1 = bf16[4,128,2560]{2,1,0:T(8,128)(2,1)} custom-call(s32[8]{0:T(128)} %pad_add_fusion.meta_ref.meta, bf16[1024,1024]{1,0:T(8,128)(2,1)} %bitcast.108, bf16[1024,1024]{1,0:T(8,128)(2,1)} %bitcast.109, bf16[1024,1024]{1,0:T(8,128)(2,1)} %bitcast.110, bf16[1024,1024]{1,0:T(8,128)(2,1)} %bitcast.111, bf16[1024,1024]{1,0:T(8,128)(2,1)} %bitcast.91, ...), custom_call_target="tpu_custom_call" | custom-call | flops 10000000000 | bytes 1000000 | tf_op jit(solution)/shard_map/gb_away/pallas_call | solution.py:581
  387.5 20.8 %attend_back.3 = (bf16[3,4,2,128,512]{4,3,2,1,0:T(8,128)(2,1)S(1)}, f32[3,2,8,512]{3,2,1,0:T(8,128)S(1)}) custom-call(s32[8]{0:T(128)S(1)} %copy-done.2, bf16[4,2,128,3072]{3,2,1,0:T(8,128)(2,1)} %bitcast.162, bf16[4,2,128,3072]{3,2,1,0:T(8,128)(2,1)} %bitcast.163, bf16[4,2,128,3072]{3,2,1,0:T(8,128)(2,1)} %bitcast.164, ...), custom_call_target="tpu_custom_call" | custom-call | flops 20999999488 | bytes 1000000 | tf_op jit(solution)/shard_map/attend_back/pallas_call | solution.py:447
  425.7 13.9 %input.1 = bf16[1024,1024]{1,0:T(8,128)(2,1)} custom-call(s32[8]{0:T(128)} %pad_add_fusion.meta_ref.meta, bf16[3,1024,512]{2,1,0:T(8,128)(2,1)} %bitcast.85, bf16[3,1024,512]{2,1,0:T(8,128)(2,1)} %bitcast.88, f32[1024,1024]{1,0:T(8,128)} %get-tuple-element.245.refs_2_, bf16[4,144,3072]{2,1,0:T(8,128)(2,1)} %copy-done.10, ...), custom_call_target="tpu_custom_call" | custom-call | flops 14000000000 | bytes 1000000 | tf_op jit(solution)/shard_map/input/pallas_call | solution.py:236
  452.8 12.1 %gb_keep.1 = (bf16[128,2560]{1,0:T(8,128)(2,1)}, bf16[128,2560]{1,0:T(8,128)(2,1)}, bf16[128,2560]{1,0:T(8,128)(2,1)}, bf16[128,1280]{1,0:T(8,128)(2,1)}, bf16[128,1280]{1,0:T(8,128)(2,1)}) custom-call(s32[8]{0:T(128)} %pad_add_fusion.meta_ref.meta, bf16[1024,1024]{1,0:T(8,128)(2,1)} %bitcast.116, bf16[1024,1024]{1,0:T(8,128)(2,1)} %bitcast.117, ...), custom_call_target="tpu_custom_call" | custom-call | flops 10000000000 | bytes 1000000 | tf_op jit(solution)/shard_map/gb_keep/pallas_call | solution.py:581
  467.0 8.1 %gc_keep.1 = (bf16[144,1536]{1,0:T(8,128)(2,1)}, bf16[144,1536]{1,0:T(8,128)(2,1)}, bf16[144,1536]{1,0:T(8,128)(2,1)}, bf16[144,768]{1,0:T(8,128)(2,1)}, bf16[144,768]{1,0:T(8,128)(2,1)}) custom-call(s32[8]{0:T(128)} %pad_add_fusion.meta_ref.meta, bf16[1024,1024]{1,0:T(8,128)(2,1)} %bitcast.120, bf16[1024,1024]{1,0:T(8,128)(2,1)} %bitcast.121, ...), custom_call_target="tpu_custom_call" | custom-call | flops 8000000000 | bytes 1000000 | tf_op jit(solution)/shard_map/gc_keep/pallas_call | solution.py:581
  485.7 12.6 %collective-permute-start.46 = (bf16[2,128,1024]{2,1,0:T(8,128)(2,1)S(1)}, bf16[2,128,1024]{2,1,0:T(8,128)(2,1)S(1)}, u32[]{:S(2)}, u32[]{:S(2)}) collective-permute-start(bf16[2,128,1024]{2,1,0:T(8,128)(2,1)S(1)} %get-tuple-element.299), channel_id=1, source_target_pairs={{0,2},{1,3},{2,0},{3,1},{4,6},{5,7},{6,4},{7,5},{8,10},{9,11},{10,... | collective-permute-start | bytes 1572872 | tf_op jit(solution)/shard_map/ppermute | solution.py:28
  521.6 11.4 %collective-permute-done.46 = bf16[2,128,1024]{2,1,0:T(8,128)(2,1)S(1)} collective-permute-done((bf16[2,128,1024]{2,1,0:T(8,128)(2,1)S(1)}, bf16[2,128,1024]{2,1,0:T(8,128)(2,1)S(1)}, u32[]{:S(2)}, u32[]{:S(2)}) %collective-permute-start.46) | collective-permute-done | bytes 524320 | tf_op jit(solution)/shard_map/ppermute | solution.py:28
  535.3 11.0 %collective-permute-start.51 = (bf16[2,128,1024]{2,1,0:T(8,128)(2,1)S(1)}, bf16[2,128,1024]{2,1,0:T(8,128)(2,1)S(1)}, u32[]{:S(2)}, u32[]{:S(2)}) collective-permute-start(bf16[2,128,1024]{2,1,0:T(8,128)(2,1)S(1)} %constant_dynamic-slice_fusion), channel_id=1, source_target_pairs={{0,1},{1,0},{2,3},{3,2},{4,5},{5,4},{6,7},{7,6},{8,9},{9,8},{10,11... | collective-permute-start | bytes 1572872 | tf_op jit(solution)/shard_map/ppermute | solution.py:28
  550.5 10.0 %collective-permute-done.50 = bf16[128,4096]{1,0:T(8,128)(2,1)S(1)} collective-permute-done((bf16[128,4096]{1,0:T(8,128)(2,1)S(1)}, bf16[128,4096]{1,0:T(8,128)(2,1)S(1)}, u32[]{:S(2)}, u32[]{:S(2)}) %collective-permute-start.50) | collective-permute-done | bytes 1048608 | tf_op jit(solution)/shard_map/ppermute | solution.py:125
  571.7 18.2 %collective-permute-done.52 = bf16[128,2560]{1,0:T(8,128)(2,1)S(1)} collective-permute-done((bf16[128,2560]{1,0:T(8,128)(2,1)S(1)}, bf16[128,2560]{1,0:T(8,128)(2,1)S(1)}, u32[]{:S(2)}, u32[]{:S(2)}) %collective-permute-start.52) | collective-permute-done | bytes 655392 | tf_op jit(solution)/shard_map/ppermute | solution.py:125
  (375 shorter events, 208.5 us)
Async XLA Ops:
  0.7 79.1 %all-to-all-start = ((bf16[4,2,128,1024]{3,2,1,0:T(8,128)(2,1)}), bf16[4,2,128,1024]{3,2,1,0:T(8,128)(2,1)S(1)}, u32[]{:S(2)}, u32[]{:S(2)}) async-start(bf16[4,2,128,1024]{3,2,1,0:T(8,128)(2,1)} %bitcast.105), calls=%async_computation | async-start | bytes 4194304 | tf_op jit(solution)/shard_map/all_to_all | solution.py:135
  9.0 69.6 %collective-permute-start.3 = (bf16[128,5120]{1,0:T(8,128)(2,1)}, bf16[128,5120]{1,0:T(8,128)(2,1)}, u32[]{:S(2)}, u32[]{:S(2)}) collective-permute-start(bf16[128,5120]{1,0:T(8,128)(2,1)} %constant_dynamic-update-slice_fusion), channel_id=1, source_target_pairs={{0,8},{4,12},{8,0},{12,4},{16,24},{20,28},{24,16},{28,20},{1,9},{5... | collective-permute-start | bytes 3932168 | tf_op jit(solution)/shard_map/ppermute | solution.py:28
  10.5 69.3 %collective-permute-start.4 = (bf16[128,5120]{1,0:T(8,128)(2,1)}, bf16[128,5120]{1,0:T(8,128)(2,1)S(1)}, u32[]{:S(2)}, u32[]{:S(2)}) collective-permute-start(bf16[128,5120]{1,0:T(8,128)(2,1)} %constant_dynamic-update-slice_fusion), channel_id=1, source_target_pairs={{0,16},{4,20},{8,24},{12,28},{16,0},{20,4},{24,8},{28,12},{1,17},{... | collective-permute-start | bytes 3932168 | tf_op jit(solution)/shard_map/ppermute | solution.py:28
  15.8 44.0 %collective-permute-start = (bf16[144,3072]{1,0:T(8,128)(2,1)}, bf16[144,3072]{1,0:T(8,128)(2,1)S(1)}, u32[]{:S(2)}, u32[]{:S(2)}) collective-permute-start(bf16[144,3072]{1,0:T(8,128)(2,1)} %fusion.1), channel_id=1, source_target_pairs={{0,8},{4,12},{8,0},{12,4},{16,24},{20,28},{24,16},{28,20},{1,9},{5... | collective-permute-start | bytes 2654216 | tf_op jit(solution)/shard_map/ppermute | solution.py:28
  16.4 62.2 %collective-permute-start.1 = (bf16[144,3072]{1,0:T(8,128)(2,1)}, bf16[144,3072]{1,0:T(8,128)(2,1)S(1)}, u32[]{:S(2)}, u32[]{:S(2)}) collective-permute-start(bf16[144,3072]{1,0:T(8,128)(2,1)} %fusion.1), channel_id=1, source_target_pairs={{0,16},{4,20},{8,24},{12,28},{16,0},{20,4},{24,8},{28,12},{1,17},{... | collective-permute-start | bytes 2654216 | tf_op jit(solution)/shard_map/ppermute | solution.py:28
  16.9 61.7 %collective-permute-start.2 = (bf16[144,3072]{1,0:T(8,128)(2,1)}, bf16[144,3072]{1,0:T(8,128)(2,1)S(1)}, u32[]{:S(2)}, u32[]{:S(2)}) collective-permute-start(bf16[144,3072]{1,0:T(8,128)(2,1)} %fusion.1), channel_id=1, source_target_pairs={{0,24},{4,28},{8,16},{12,20},{16,8},{20,12},{24,0},{28,4},{1,25},{... | collective-permute-start | bytes 2654216 | tf_op jit(solution)/shard_map/ppermute | solution.py:28
  119.4 32.0 %collective-permute-start.9 = (bf16[4,128,5120]{2,1,0:T(8,128)(2,1)}, bf16[4,128,5120]{2,1,0:T(8,128)(2,1)}, u32[]{:S(2)}, u32[]{:S(2)}) collective-permute-start(bf16[4,128,5120]{2,1,0:T(8,128)(2,1)} %pad_maximum_fusion.refs_5_.refs_2_.refs_7_), channel_id=1, source_target_pairs={{0,4},{4,0},{8,12},{12,8},{16,20},{20,16},{24,28},{28,24},{1,5},{5... | collective-permute-start | bytes 15728648 | tf_op jit(solution)/shard_map/ppermute | solution.py:28
  119.4 32.0 %collective-permute-start.10 = (bf16[512,1024]{1,0:T(8,128)(2,1)S(1)}, bf16[512,1024]{1,0:T(8,128)(2,1)S(1)}, u32[]{:S(2)}, u32[]{:S(2)}) collective-permute-start(bf16[512,1024]{1,0:T(8,128)(2,1)S(1)} %copy-done.32), channel_id=1, source_target_pairs={{0,8},{4,12},{8,0},{12,4},{16,24},{20,28},{24,16},{28,20},{1,9},{5... | collective-permute-start | bytes 3145736 | tf_op jit(solution)/shard_map/ppermute | solution.py:28
  121.0 30.5 %collective-permute-start.11 = (bf16[512,1024]{1,0:T(8,128)(2,1)S(1)}, bf16[512,1024]{1,0:T(8,128)(2,1)S(1)}, u32[]{:S(2)}, u32[]{:S(2)}) collective-permute-start(bf16[512,1024]{1,0:T(8,128)(2,1)S(1)} %copy-done.32), channel_id=1, source_target_pairs={{0,16},{4,20},{8,24},{12,28},{16,0},{20,4},{24,8},{28,12},{1,17},{... | collective-permute-start | bytes 3145736 | tf_op jit(solution)/shard_map/ppermute | solution.py:28
  122.6 28.9 %collective-permute-start.12 = (bf16[2,128,1024]{2,1,0:T(8,128)(2,1)S(1)}, bf16[2,128,1024]{2,1,0:T(8,128)(2,1)S(1)}, u32[]{:S(2)}, u32[]{:S(2)}) collective-permute-start(bf16[2,128,1024]{2,1,0:T(8,128)(2,1)S(1)} %constant_dynamic-slice_fusion.7), channel_id=1, source_target_pairs={{0,2},{1,3},{2,0},{3,1},{4,6},{5,7},{6,4},{7,5},{8,10},{9,11},{10,... | collective-permute-start | bytes 1572872 | tf_op jit(solution)/shard_map/ppermute | solution.py:28
  228.8 28.9 %collective-permute-start.17 = (bf16[4,512,1024]{2,1,0:T(8,128)(2,1)}, bf16[4,512,1024]{2,1,0:T(8,128)(2,1)}, u32[]{:S(2)}, u32[]{:S(2)}) collective-permute-start(bf16[4,512,1024]{2,1,0:T(8,128)(2,1)} %gd_away.1), channel_id=1, source_target_pairs={{0,4},{4,0},{8,12},{12,8},{16,20},{20,16},{24,28},{28,24},{1,5},{5... | collective-permute-start | bytes 12582920 | tf_op jit(solution)/shard_map/ppermute | solution.py:28
  283.5 37.5 %collective-permute-start.22 = (bf16[4,128,4096]{2,1,0:T(8,128)(2,1)}, bf16[4,128,4096]{2,1,0:T(8,128)(2,1)}, u32[]{:S(2)}, u32[]{:S(2)}) collective-permute-start(bf16[4,128,4096]{2,1,0:T(8,128)(2,1)} %gu_away.1), channel_id=1, source_target_pairs={{0,4},{4,0},{8,12},{12,8},{16,20},{20,16},{24,28},{28,24},{1,5},{5... | collective-permute-start | bytes 12582920 | tf_op jit(solution)/shard_map/ppermute | solution.py:28
  287.4 33.6 %collective-permute-start.24 = (bf16[512,1024]{1,0:T(8,128)(2,1)}, bf16[512,1024]{1,0:T(8,128)(2,1)}, u32[]{:S(2)}, u32[]{:S(2)}) collective-permute-start(bf16[512,1024]{1,0:T(8,128)(2,1)} %pad_maximum_fusion.4), channel_id=1, source_target_pairs={{0,16},{4,20},{8,24},{12,28},{16,0},{20,4},{24,8},{28,12},{1,17},{... | collective-permute-start | bytes 3145736 | tf_op jit(solution)/shard_map/ppermute | solution.py:28
  289.8 31.2 %collective-permute-start.23 = (bf16[512,1024]{1,0:T(8,128)(2,1)S(1)}, bf16[512,1024]{1,0:T(8,128)(2,1)}, u32[]{:S(2)}, u32[]{:S(2)}) collective-permute-start(bf16[512,1024]{1,0:T(8,128)(2,1)S(1)} %pad_maximum_fusion.3), channel_id=1, source_target_pairs={{0,8},{4,12},{8,0},{12,4},{16,24},{20,28},{24,16},{28,20},{1,9},{5... | collective-permute-start | bytes 3145736 | tf_op jit(solution)/shard_map/ppermute | solution.py:28
  292.2 28.8 %collective-permute-start.25 = (bf16[2,128,1024]{2,1,0:T(8,128)(2,1)}, bf16[2,128,1024]{2,1,0:T(8,128)(2,1)S(1)}, u32[]{:S(2)}, u32[]{:S(2)}) collective-permute-start(bf16[2,128,1024]{2,1,0:T(8,128)(2,1)} %constant_dynamic-slice_fusion.3), channel_id=1, source_target_pairs={{0,3},{1,2},{2,1},{3,0},{4,7},{5,6},{6,5},{7,4},{8,11},{9,10},{10,... | collective-permute-start | bytes 1572872 | tf_op jit(solution)/shard_map/ppermute | solution.py:28
  324.0 41.1 %collective-permute-start.26 = (bf16[512,1024]{1,0:T(8,128)(2,1)S(1)}, bf16[512,1024]{1,0:T(8,128)(2,1)}, u32[]{:S(2)}, u32[]{:S(2)}) collective-permute-start(bf16[512,1024]{1,0:T(8,128)(2,1)S(1)} %add_convert_fusion.5), channel_id=1, source_target_pairs={{0,1},{3,2},{4,5},{7,6},{8,9},{11,10},{12,13},{15,14},{16,17},{19,... | collective-permute-start | bytes 3145736 | tf_op jit(solution)/shard_map/ppermute | solution.py:117
  376.7 34.8 %collective-permute-start.29 = (bf16[4,128,2560]{2,1,0:T(8,128)(2,1)}, bf16[4,128,2560]{2,1,0:T(8,128)(2,1)}, u32[]{:S(2)}, u32[]{:S(2)}) collective-permute-start(bf16[4,128,2560]{2,1,0:T(8,128)(2,1)} %gb_away.1), channel_id=1, source_target_pairs={{0,4},{4,0},{8,12},{12,8},{16,20},{20,16},{24,28},{28,24},{1,5},{5... | collective-permute-start | bytes 7864328 | tf_op jit(solution)/shard_map/ppermute | solution.py:28
  378.5 32.5 %collective-permute-start.32 = (bf16[512,1024]{1,0:T(8,128)(2,1)S(1)}, bf16[512,1024]{1,0:T(8,128)(2,1)}, u32[]{:S(2)}, u32[]{:S(2)}) collective-permute-start(bf16[512,1024]{1,0:T(8,128)(2,1)S(1)} %add_convert_fusion.4), channel_id=1, source_target_pairs={{1,2},{2,1},{5,6},{6,5},{9,10},{10,9},{13,14},{14,13},{17,18},{18,... | collective-permute-start | bytes 3145736 | tf_op jit(solution)/shard_map/ppermute | solution.py:121
  419.3 32.5 %collective-permute-start.35 = (bf16[4,144,1536]{2,1,0:T(8,128)(2,1)}, bf16[4,144,1536]{2,1,0:T(8,128)(2,1)S(1)}, u32[]{:S(2)}, u32[]{:S(2)}) collective-permute-start(bf16[4,144,1536]{2,1,0:T(8,128)(2,1)} %gc_away.1), channel_id=1, source_target_pairs={{0,4},{4,0},{8,12},{12,8},{16,20},{20,16},{24,28},{28,24},{1,5},{5... | collective-permute-start | bytes 5308424 | tf_op jit(solution)/shard_map/ppermute | solution.py:28
  485.7 47.3 %collective-permute-start.46 = (bf16[2,128,1024]{2,1,0:T(8,128)(2,1)S(1)}, bf16[2,128,1024]{2,1,0:T(8,128)(2,1)S(1)}, u32[]{:S(2)}, u32[]{:S(2)}) collective-permute-start(bf16[2,128,1024]{2,1,0:T(8,128)(2,1)S(1)} %get-tuple-element.299), channel_id=1, source_target_pairs={{0,2},{1,3},{2,0},{3,1},{4,6},{5,7},{6,4},{7,5},{8,10},{9,11},{10,... | collective-permute-start | bytes 1572872 | tf_op jit(solution)/shard_map/ppermute | solution.py:28
  498.2 36.1 %collective-permute-start.47 = (bf16[2,128,1024]{2,1,0:T(8,128)(2,1)S(1)}, bf16[2,128,1024]{2,1,0:T(8,128)(2,1)S(1)}, u32[]{:S(2)}, u32[]{:S(2)}) collective-permute-start(bf16[2,128,1024]{2,1,0:T(8,128)(2,1)S(1)} %get-tuple-element.298), channel_id=1, source_target_pairs={{0,3},{1,2},{2,1},{3,0},{4,7},{5,6},{6,5},{7,4},{8,11},{9,10},{10,... | collective-permute-start | bytes 1572872 | tf_op jit(solution)/shard_map/ppermute | solution.py:28
  504.0 30.3 %collective-permute-start.45 = (bf16[128,2560]{1,0:T(8,128)(2,1)S(1)}, bf16[128,2560]{1,0:T(8,128)(2,1)S(1)}, u32[]{:S(2)}, u32[]{:S(2)}) collective-permute-start(bf16[128,2560]{1,0:T(8,128)(2,1)S(1)} %add_convert_fusion.8), channel_id=1, source_target_pairs={{0,1},{3,2},{4,5},{7,6},{8,9},{11,10},{12,13},{15,14},{16,17},{19,... | collective-permute-start | bytes 1966088 | tf_op jit(solution)/shard_map/ppermute | solution.py:117
  534.5 31.6 %collective-permute-start.48 = (bf16[128,2560]{1,0:T(8,128)(2,1)S(1)}, bf16[128,2560]{1,0:T(8,128)(2,1)S(1)}, u32[]{:S(2)}, u32[]{:S(2)}) collective-permute-start(bf16[128,2560]{1,0:T(8,128)(2,1)S(1)} %add_convert_fusion.7), channel_id=1, source_target_pairs={{1,2},{2,1},{5,6},{6,5},{9,10},{10,9},{13,14},{14,13},{17,18},{18,... | collective-permute-start | bytes 1966088 | tf_op jit(solution)/shard_map/ppermute | solution.py:121
  535.3 30.9 %collective-permute-start.51 = (bf16[2,128,1024]{2,1,0:T(8,128)(2,1)S(1)}, bf16[2,128,1024]{2,1,0:T(8,128)(2,1)S(1)}, u32[]{:S(2)}, u32[]{:S(2)}) collective-permute-start(bf16[2,128,1024]{2,1,0:T(8,128)(2,1)S(1)} %constant_dynamic-slice_fusion), channel_id=1, source_target_pairs={{0,1},{1,0},{2,3},{3,2},{4,5},{5,4},{6,7},{7,6},{8,9},{9,8},{10,11... | collective-permute-start | bytes 1572872 | tf_op jit(solution)/shard_map/ppermute | solution.py:28
  (97 other events, 1266.9 us)
